TPU v7x, 32 devices: a whole 2x2x4 slice. The times are simulated.
32 devices in a mesh: section: 2 (over y), dp: 2 (over x), seq: 8 (over z, core).
Axes of the slice: x: 2, y: 2, z: 4, core: 2. Of those that a mesh axis runs over, the one named last changes fastest.
Arguments:
- ends: bfloat16 [2, 8, 1024, 960], P('section', 'dp', 'seq'), may hold values from -6 to 6
- segments: int32 [8, 1024], P('dp', 'seq'), may hold values from 0 to 7, as said below
- positions: int32 [8, 1024], P('dp', 'seq'), may hold values from 0 to 1023, as said below
- query_weights: bfloat16 [2, 960, 960], P('section', 'dp', 'seq'), may hold values from -0.1875 to 0.1875
- key_weights: bfloat16 [2, 960, 320], P('section', 'dp', 'seq'), may hold values from -0.1875 to 0.1875
- value_weights: bfloat16 [2, 960, 320], P('section', 'dp', 'seq'), may hold values from -0.1875 to 0.1875
- out_weights: bfloat16 [2, 960, 960], P('section', 'seq', 'dp'), may hold values from -1.25 to 1.25
- gate_weights: bfloat16 [2, 960, 2560], P('section', 'dp', 'seq'), may hold values from -0.1875 to 0.1875
- up_weights: bfloat16 [2, 960, 2560], P('section', 'dp', 'seq'), may hold values from -0.1875 to 0.1875
- down_weights: bfloat16 [2, 2560, 960], P('section', 'seq', 'dp'), may hold values from -0.125 to 0.125
- norm_gains: bfloat16 [2, 2, 960], P('section', None, 'seq'), may hold values from 0.099609375 to 1.8984375
Outputs:
- activations: bfloat16 [2, 8, 1024, 960], P('section', 'dp', 'seq')
- input_grads: bfloat16 [2, 8, 1024, 960], P('section', 'dp', 'seq')
- query_grad: float32 [2, 960, 960], P('section', 'dp', 'seq')
- key_grad: float32 [2, 960, 320], P('section', 'dp', 'seq')
- value_grad: float32 [2, 960, 320], P('section', 'dp', 'seq')
- out_grad: float32 [2, 960, 960], P('section', 'seq', 'dp')
- gate_grad: float32 [2, 960, 2560], P('section', 'dp', 'seq')
- up_grad: float32 [2, 960, 2560], P('section', 'dp', 'seq')
- down_grad: float32 [2, 2560, 960], P('section', 'seq', 'dp')
- gain_grad: float32 [2, 2, 960], P('section', None, 'seq')
Inputs may be any that keep to these rules, and one draw needn't show every extreme that they name: `segments`: within each sequence the ids start at 0 and rise by 0 or 1 from one position to the next, so equal ids form one document; among the 4 sequences of each index of dp, one is a single document and another holds 8 documents. `positions`: 0 at a document's first token, rising by 1 a token within it.
All inputs are finite; a program needn't handle non-finite values.
Results may differ from a plain program's by a relative error of at most 0.025.
Values may be sent and summed in bfloat16 or wider, within the bound.
A program may use at most 256 MiB of HBM per device.

v0:
```python
import math

import jax
import jax.numpy as jnp
from jax import lax
from jax.sharding import PartitionSpec as P

D = 960
HEADS = 15
KV_HEADS = 5
HEAD_DIM = 64
SEQ_MB = 2


EPS = 1e-05
THETA = 100000.0
MASKED = -1e30


def shifted(value, axis, steps):
    count = lax.axis_size(axis)
    leading, last = (max(0, -steps), min(count, count - steps))
    return lax.ppermute(value, axis, [(source, source + steps) for source in range(leading, last)])


def rope_tables(positions):
    half_size = HEAD_DIM // 2
    exponent = jnp.arange(half_size, dtype=jnp.float32) * (2.0 / HEAD_DIM)
    frequency = jnp.exp(-exponent * math.log(THETA))
    angles = positions.astype(jnp.float32)[..., None] * frequency
    return (jnp.cos(angles), jnp.sin(angles))


def rotate(values, cosine, sine):
    front, back = jnp.split(values, 2, axis=-1)
    cosine = cosine[..., None, :]
    sine = sine[..., None, :]
    return jnp.concatenate([front * cosine - back * sine, back * cosine + front * sine], axis=-1)


def unrotate(gradient, cosine, sine):
    front, back = jnp.split(gradient, 2, axis=-1)
    cosine = cosine[..., None, :]
    sine = sine[..., None, :]
    return jnp.concatenate([front * cosine + back * sine, back * cosine - front * sine], axis=-1)


def inner_rows(left, right):
    return lax.dot_general(
        left, right, (((0,), (0,)), ((), ())), preferred_element_type=jnp.float32
    )


def against(left, weight):
    return lax.dot_general(
        left, weight, (((1,), (1,)), ((), ())), preferred_element_type=jnp.float32
    )


def normalize(values, gain):
    scale = lax.rsqrt(jnp.mean(values * values, axis=-1, keepdims=True) + EPS)
    return (scale, (values * scale * gain).astype(jnp.bfloat16))


def norm_back(gradient, values, scale, gain):
    weighted = gradient * gain
    inward = scale * weighted - values * (scale * scale * scale) * jnp.mean(
        weighted * values, axis=-1, keepdims=True
    )
    return (inward, jnp.sum(gradient * values * scale, axis=0))


def key_slice(gathered, segment_all, begin, width):
    count = gathered.shape[0]
    key_width = KV_HEADS * HEAD_DIM
    block = lax.dynamic_slice_in_dim(gathered, begin, width, 1)
    segment_block = lax.dynamic_slice_in_dim(segment_all, begin, width, 1)
    keys = block[..., :key_width].reshape(count, width, KV_HEADS, HEAD_DIM)
    values = block[..., key_width:].reshape(count, width, KV_HEADS, HEAD_DIM)
    return (keys, values, segment_block)


def masked_scores(query_view, keys, segment_block, segment_mark, query_index, begin):
    width = keys.shape[1]
    scores = jnp.einsum(
        "sqgrd,skgd->sgrqk", query_view, keys, preferred_element_type=jnp.float32
    ) * HEAD_DIM ** (-0.5)
    key_index = begin + jnp.arange(width)
    allowed = (key_index[None, None, :] <= query_index[None, :, None]) & (
        segment_block[:, None, :] == segment_mark[:, :, None]
    )
    return jnp.where(allowed[:, None, None], scores, MASKED)


def block_width():
    return 512


def attend(query_view, gathered, segment_all, segment_mark, query_index):
    count, local_length, groups, ratio, head_size = query_view.shape
    key_length = gathered.shape[1]
    width = block_width()
    blocks = key_length // width
    row_shape = (count, groups, ratio, local_length)

    def measure(index, carry):
        top, total = carry
        begin = index * width
        keys, values, segment_block = key_slice(gathered, segment_all, begin, width)
        scores = masked_scores(query_view, keys, segment_block, segment_mark, query_index, begin)
        new_top = jnp.maximum(top, jnp.max(scores, axis=-1))
        total = total * jnp.exp(top - new_top) + jnp.sum(
            jnp.exp(scores - new_top[..., None]), axis=-1
        )
        return (new_top, total)

    start = (jnp.full(row_shape, MASKED, jnp.float32), jnp.zeros(row_shape, jnp.float32))
    top, total = lax.fori_loop(0, blocks, measure, start)
    log_total = top + jnp.log(total)

    def gather_mix(index, running):
        begin = index * width
        keys, values, segment_block = key_slice(gathered, segment_all, begin, width)
        scores = masked_scores(query_view, keys, segment_block, segment_mark, query_index, begin)
        shares = jnp.exp(scores - log_total[..., None]).astype(jnp.bfloat16)
        return running + jnp.einsum(
            "sgrqk,skgd->sqgrd", shares, values, preferred_element_type=jnp.float32
        )

    mixed = lax.fori_loop(0, blocks, gather_mix, jnp.zeros(query_view.shape, jnp.float32))
    return (mixed, log_total)


def attend_back(
    query_view, gathered, segment_all, segment_mark, query_index, log_total, back_view, delta
):
    count = query_view.shape[0]
    key_length = gathered.shape[1]
    key_width = KV_HEADS * HEAD_DIM
    width = block_width()
    blocks = key_length // width
    scale = HEAD_DIM ** (-0.5)

    def sweep(index, carry):
        back_query, buffer = carry
        begin = index * width
        keys, values, segment_block = key_slice(gathered, segment_all, begin, width)
        scores = masked_scores(query_view, keys, segment_block, segment_mark, query_index, begin)
        shares = jnp.exp(scores - log_total[..., None])
        back_shares = jnp.einsum(
            "sqgrd,skgd->sgrqk", back_view, values, preferred_element_type=jnp.float32
        )
        back_scores = (shares * (back_shares - delta[..., None])).astype(jnp.bfloat16)
        back_values = jnp.einsum(
            "sgrqk,sqgrd->skgd",
            shares.astype(jnp.bfloat16),
            back_view,
            preferred_element_type=jnp.float32,
        )
        back_keys = (
            jnp.einsum(
                "sgrqk,sqgrd->skgd", back_scores, query_view, preferred_element_type=jnp.float32
            )
            * scale
        )
        back_query = (
            back_query
            + jnp.einsum("sgrqk,skgd->sqgrd", back_scores, keys, preferred_element_type=jnp.float32)
            * scale
        )
        piece = jnp.concatenate(
            [
                back_keys.reshape(count, width, key_width),
                back_values.reshape(count, width, key_width),
            ],
            axis=-1,
        )
        return (back_query, lax.dynamic_update_slice_in_dim(buffer, piece, begin, 1))

    start = (
        jnp.zeros(query_view.shape, jnp.float32),
        jnp.zeros((count, key_length, 2 * key_width), jnp.float32),
    )
    return lax.fori_loop(0, blocks, sweep, start)


def layer_forward(hidden, full, segment_local, cosine, sine, query_index):
    (
        query_weight,
        key_weight,
        value_weight,
        out_weight,
        gate_weight,
        up_weight,
        down_weight,
        gains,
    ) = full
    count, local_length = segment_local.shape
    rows = hidden.shape[0]
    key_width = KV_HEADS * HEAD_DIM
    scale_front, normed = normalize(hidden, gains[0].astype(jnp.float32))
    queries = jnp.dot(normed, query_weight, preferred_element_type=jnp.float32)
    keys = jnp.dot(normed, key_weight, preferred_element_type=jnp.float32)
    values = jnp.dot(normed, value_weight, preferred_element_type=jnp.float32).astype(jnp.bfloat16)
    turned_queries = rotate(queries.reshape(rows, HEADS, HEAD_DIM), cosine, sine).astype(
        jnp.bfloat16
    )
    turned_keys = rotate(keys.reshape(rows, KV_HEADS, HEAD_DIM), cosine, sine).astype(jnp.bfloat16)
    packed = jnp.concatenate(
        [
            turned_keys.reshape(count, local_length, key_width),
            values.reshape(count, local_length, key_width),
        ],
        axis=-1,
    )
    segment_mark = segment_local.astype(jnp.bfloat16)
    gathered, segment_all = (
        lax.all_gather(packed, "seq", axis=1, tiled=True),
        lax.all_gather(segment_mark, "seq", axis=1, tiled=True),
    )
    query_view = turned_queries.reshape(count, local_length, KV_HEADS, HEADS // KV_HEADS, HEAD_DIM)
    mixed, log_total = attend(query_view, gathered, segment_all, segment_mark, query_index)
    mixed_low = mixed.reshape(rows, HEADS * HEAD_DIM).astype(jnp.bfloat16)
    middle = hidden + jnp.dot(mixed_low, out_weight, preferred_element_type=jnp.float32)
    scale_back, normed_back = normalize(middle, gains[1].astype(jnp.float32))
    gate = jnp.dot(normed_back, gate_weight, preferred_element_type=jnp.float32)
    upward = jnp.dot(normed_back, up_weight, preferred_element_type=jnp.float32)
    product = (gate * jax.nn.sigmoid(gate) * upward).astype(jnp.bfloat16)
    output = middle + jnp.dot(product, down_weight, preferred_element_type=jnp.float32)
    kept = (
        hidden,
        scale_front,
        normed,
        query_view,
        gathered,
        segment_all,
        mixed,
        log_total,
        mixed_low,
        middle,
        scale_back,
        normed_back,
        gate,
        upward,
        product,
    )
    return (output, kept)


def layer_backward(incoming, full, kept, segment_local, cosine, sine, query_index):
    (
        query_weight,
        key_weight,
        value_weight,
        out_weight,
        gate_weight,
        up_weight,
        down_weight,
        gains,
    ) = full
    (
        hidden,
        scale_front,
        normed,
        query_view,
        gathered,
        segment_all,
        mixed,
        log_total,
        mixed_low,
        middle,
        scale_back,
        normed_back,
        gate,
        upward,
        product,
    ) = kept
    rows = hidden.shape[0]
    key_width = KV_HEADS * HEAD_DIM
    gain_front = gains[0].astype(jnp.float32)
    gain_back = gains[1].astype(jnp.float32)
    incoming_low = incoming.astype(jnp.bfloat16)
    down_grad = inner_rows(product, incoming_low)
    back_product = against(incoming_low, down_weight)
    sigma = jax.nn.sigmoid(gate)
    back_gate = (back_product * upward * sigma * (1.0 + gate * (1.0 - sigma))).astype(jnp.bfloat16)
    back_up = (back_product * gate * sigma).astype(jnp.bfloat16)
    gate_grad = inner_rows(normed_back, back_gate)
    up_grad = inner_rows(normed_back, back_up)
    back_normed = against(back_gate, gate_weight) + against(back_up, up_weight)
    inward, gain_back_grad = norm_back(back_normed, middle, scale_back, gain_back)
    back_middle = incoming + inward
    branch = back_middle.astype(jnp.bfloat16)
    out_grad = inner_rows(mixed_low, branch)
    back_mixed = against(branch, out_weight).astype(jnp.bfloat16)
    back_view = back_mixed.reshape(query_view.shape)
    delta = jnp.einsum("sqgrd,sqgrd->sgrq", back_view.astype(jnp.float32), mixed)
    segment_mark = segment_local.astype(jnp.bfloat16)
    back_query, buffer = attend_back(
        query_view, gathered, segment_all, segment_mark, query_index, log_total, back_view, delta
    )
    summed = lax.psum_scatter(
        buffer.astype(jnp.bfloat16), "seq", scatter_dimension=1, tiled=True
    ).astype(jnp.float32)
    back_turned_keys = summed[..., :key_width].reshape(rows, KV_HEADS, HEAD_DIM)
    back_values = summed[..., key_width:].reshape(rows, key_width).astype(jnp.bfloat16)
    back_queries = (
        unrotate(back_query.reshape(rows, HEADS, HEAD_DIM), cosine, sine)
        .reshape(rows, HEADS * HEAD_DIM)
        .astype(jnp.bfloat16)
    )
    back_keys = (
        unrotate(back_turned_keys, cosine, sine).reshape(rows, key_width).astype(jnp.bfloat16)
    )
    query_grad = inner_rows(normed, back_queries)
    key_grad = inner_rows(normed, back_keys)
    value_grad = inner_rows(normed, back_values)
    back_front = (
        against(back_queries, query_weight)
        + against(back_keys, key_weight)
        + against(back_values, value_weight)
    )
    inward_front, gain_front_grad = norm_back(back_front, hidden, scale_front, gain_front)
    back_hidden = back_middle + inward_front
    gains_grad = jnp.stack([gain_front_grad, gain_back_grad])
    return (
        back_hidden,
        (query_grad, key_grad, value_grad, out_grad, gate_grad, up_grad, down_grad, gains_grad),
    )


def gather_weights(shards):
    query_part, key_part, value_part, out_part, gate_part, up_part, down_part, gain_part = shards
    wide = (
        lax.all_gather(query_part, "seq", axis=1, tiled=True),
        lax.all_gather(key_part, "seq", axis=1, tiled=True),
        lax.all_gather(value_part, "seq", axis=1, tiled=True),
        lax.all_gather(out_part, "seq", axis=0, tiled=True),
        lax.all_gather(gate_part, "seq", axis=1, tiled=True),
        lax.all_gather(up_part, "seq", axis=1, tiled=True),
        lax.all_gather(down_part, "seq", axis=0, tiled=True),
        lax.all_gather(gain_part, "seq", axis=1, tiled=True),
    )
    whole = (
        lax.all_gather(wide[0], "dp", axis=0, tiled=True),
        lax.all_gather(wide[1], "dp", axis=0, tiled=True),
        lax.all_gather(wide[2], "dp", axis=0, tiled=True),
        lax.all_gather(wide[3], "dp", axis=1, tiled=True),
        lax.all_gather(wide[4], "dp", axis=0, tiled=True),
        lax.all_gather(wide[5], "dp", axis=0, tiled=True),
        lax.all_gather(wide[6], "dp", axis=1, tiled=True),
    )
    return tuple(whole) + (wide[7],)


def gather_again(shards):
    query_part, key_part, value_part, out_part, gate_part, up_part, down_part, gain_part = shards
    wide = (
        lax.all_gather(query_part, "seq", axis=1, tiled=True),
        lax.all_gather(key_part, "seq", axis=1, tiled=True),
        lax.all_gather(value_part, "seq", axis=1, tiled=True),
        lax.all_gather(out_part, "seq", axis=0, tiled=True),
        lax.all_gather(gate_part, "seq", axis=1, tiled=True),
        lax.all_gather(up_part, "seq", axis=1, tiled=True),
        lax.all_gather(down_part, "seq", axis=0, tiled=True),
        lax.all_gather(gain_part, "seq", axis=1, tiled=True),
    )
    whole = (
        lax.all_gather(wide[0], "dp", axis=0, tiled=True),
        lax.all_gather(wide[1], "dp", axis=0, tiled=True),
        lax.all_gather(wide[2], "dp", axis=0, tiled=True),
        lax.all_gather(wide[3], "dp", axis=1, tiled=True),
        lax.all_gather(wide[4], "dp", axis=0, tiled=True),
        lax.all_gather(wide[5], "dp", axis=0, tiled=True),
        lax.all_gather(wide[6], "dp", axis=1, tiled=True),
    )
    return tuple(whole) + (wide[7],)


def reduce_grads(grads):
    query_grad, key_grad, value_grad, out_grad, gate_grad, up_grad, down_grad, gains_grad = grads
    spread = jnp.broadcast_to(gains_grad[None], (lax.axis_size("dp"),) + gains_grad.shape)
    first = (
        lax.psum_scatter(
            query_grad.astype(jnp.bfloat16), "dp", scatter_dimension=0, tiled=True
        ).astype(jnp.float32),
        lax.psum_scatter(
            key_grad.astype(jnp.bfloat16), "dp", scatter_dimension=0, tiled=True
        ).astype(jnp.float32),
        lax.psum_scatter(
            value_grad.astype(jnp.bfloat16), "dp", scatter_dimension=0, tiled=True
        ).astype(jnp.float32),
        lax.psum_scatter(
            out_grad.astype(jnp.bfloat16), "dp", scatter_dimension=1, tiled=True
        ).astype(jnp.float32),
        lax.psum_scatter(
            gate_grad.astype(jnp.bfloat16), "dp", scatter_dimension=0, tiled=True
        ).astype(jnp.float32),
        lax.psum_scatter(
            up_grad.astype(jnp.bfloat16), "dp", scatter_dimension=0, tiled=True
        ).astype(jnp.float32),
        lax.psum_scatter(
            down_grad.astype(jnp.bfloat16), "dp", scatter_dimension=1, tiled=True
        ).astype(jnp.float32),
        lax.psum_scatter(spread.astype(jnp.bfloat16), "dp", scatter_dimension=0, tiled=True).astype(
            jnp.float32
        ),
    )
    second = (
        lax.psum_scatter(
            first[0].astype(jnp.bfloat16), "seq", scatter_dimension=1, tiled=True
        ).astype(jnp.float32),
        lax.psum_scatter(
            first[1].astype(jnp.bfloat16), "seq", scatter_dimension=1, tiled=True
        ).astype(jnp.float32),
        lax.psum_scatter(
            first[2].astype(jnp.bfloat16), "seq", scatter_dimension=1, tiled=True
        ).astype(jnp.float32),
        lax.psum_scatter(
            first[3].astype(jnp.bfloat16), "seq", scatter_dimension=0, tiled=True
        ).astype(jnp.float32),
        lax.psum_scatter(
            first[4].astype(jnp.bfloat16), "seq", scatter_dimension=1, tiled=True
        ).astype(jnp.float32),
        lax.psum_scatter(
            first[5].astype(jnp.bfloat16), "seq", scatter_dimension=1, tiled=True
        ).astype(jnp.float32),
        lax.psum_scatter(
            first[6].astype(jnp.bfloat16), "seq", scatter_dimension=0, tiled=True
        ).astype(jnp.float32),
        lax.psum_scatter(
            first[7][0].astype(jnp.bfloat16), "seq", scatter_dimension=1, tiled=True
        ).astype(jnp.float32),
    )
    return tuple(second)


def pick_section(section, early, late):

    def select(early_part, late_part):
        return jnp.where(section == 0, early_part, late_part)

    return jax.tree.map(select, early, late)


def add_tree(left, right):
    return jax.tree.map(jnp.add, left, right)


def on_device(
    ends,
    segments,
    positions,
    query_weights,
    key_weights,
    value_weights,
    out_weights,
    gate_weights,
    up_weights,
    down_weights,
    norm_gains,
):
    section = lax.axis_index("section")
    sections = lax.axis_size("section")
    count = SEQ_MB
    micro = segments.shape[0] // count
    local_length = segments.shape[1]
    rows = count * local_length
    ticks = micro + sections - 1
    query_index = lax.axis_index("seq") * local_length + jnp.arange(local_length)
    shards = (
        query_weights[0],
        key_weights[0],
        value_weights[0],
        out_weights[0],
        gate_weights[0],
        up_weights[0],
        down_weights[0],
        norm_gains[0],
    )
    full = gather_weights(shards)
    outside = ends[0].reshape(micro, rows, D)
    blank = jnp.zeros((rows, D), jnp.bfloat16)

    def batch_inputs(index):
        segment_local = lax.dynamic_slice_in_dim(segments, index * count, count, 0)
        place = lax.dynamic_slice_in_dim(positions, index * count, count, 0).reshape(rows)
        cosine, sine = rope_tables(place)
        return (segment_local, cosine, sine)

    received = blank
    results = []
    stores = []
    for tick in range(ticks):
        own = outside[tick] if tick < micro else blank
        source = jnp.where(section == 0, own, received)
        index = jnp.clip(tick - section, 0, micro - 1)
        segment_local, cosine, sine = batch_inputs(index)
        output, kept = layer_forward(
            source.astype(jnp.float32), full, segment_local, cosine, sine, query_index
        )
        sent = output.astype(jnp.bfloat16)
        results.append(sent)
        stores.append(kept)
        if tick + 1 < ticks:
            received = shifted(sent, "section", 1)
    back_full = gather_again(shards)
    received = blank
    sent_back = []
    totals = None
    for tick in range(ticks):
        own = outside[tick] if tick < micro else blank
        incoming = jnp.where(section == sections - 1, own, received)
        index = jnp.clip(tick - 1 + section, 0, micro - 1)
        segment_local, cosine, sine = batch_inputs(index)
        kept = pick_section(section, stores[max(tick - 1, 0)], stores[min(tick + 1, ticks - 1)])
        back_hidden, grads = layer_backward(
            incoming.astype(jnp.float32), back_full, kept, segment_local, cosine, sine, query_index
        )
        sent = back_hidden.astype(jnp.bfloat16)
        sent_back.append(sent)
        reduced = reduce_grads(grads)
        totals = reduced if totals is None else add_tree(totals, reduced)
        if tick + 1 < ticks:
            received = shifted(sent, "section", -1)
    outputs_list = []
    grads_list = []
    for batch in range(micro):
        outputs_list.append(
            jnp.where(section == 0, results[batch], results[batch + 1]).reshape(
                count, local_length, D
            )
        )
        grads_list.append(
            jnp.where(section == 0, sent_back[batch + 1], sent_back[batch]).reshape(
                count, local_length, D
            )
        )
    activations = jnp.concatenate(outputs_list, axis=0)[None]
    input_grads = jnp.concatenate(grads_list, axis=0)[None]
    return (
        activations,
        input_grads,
        totals[0][None],
        totals[1][None],
        totals[2][None],
        totals[3][None],
        totals[4][None],
        totals[5][None],
        totals[6][None],
        totals[7][None],
    )


def solution(mesh):
    return jax.shard_map(
        on_device,
        mesh=mesh,
        in_specs=(
            P("section", "dp", "seq", None),
            P("dp", "seq"),
            P("dp", "seq"),
            P("section", "dp", "seq"),
            P("section", "dp", "seq"),
            P("section", "dp", "seq"),
            P("section", "seq", "dp"),
            P("section", "dp", "seq"),
            P("section", "dp", "seq"),
            P("section", "seq", "dp"),
            P("section", None, "seq"),
        ),
        out_specs=(
            P("section", "dp", "seq", None),
            P("section", "dp", "seq", None),
            P("section", "dp", "seq"),
            P("section", "dp", "seq"),
            P("section", "dp", "seq"),
            P("section", "seq", "dp"),
            P("section", "dp", "seq"),
            P("section", "dp", "seq"),
            P("section", "seq", "dp"),
            P("section", None, "seq"),
        ),
        check_vma=False,
    )
```

profile of v0, /device:TPU:0, one launch (start us, length us, event | category | flops | bytes accessed | tf_op | source)
XLA Modules:
  0.0 2692.5 jit_solution(11036578286484807490)
XLA Ops:
  9.8 33.5 %all-gather.5 = bf16[1,480,960]{1,0,2:T(2,128)(2,1)S(1)} all-gather(bf16[1,480,120]{1,0,2:T(2,128)(2,1)S(1)} %copy.293), channel_id=7, replica_groups=mesh['section'=2,'dp'=2,'seq'=8] {'seq'}, dimensions={2}, use_global_device_ids=true | all-gather | bytes 1036800 | tf_op jit(solution)/shard_map/all_gather | solution.py:335
  112.0 30.2 %all-gather.2 = bf16[1,960,320]{2,0,1:T(2,128)(2,1)S(1)} all-gather(bf16[1,480,320]{2,0,1:T(2,128)(2,1)} %copy.289), channel_id=4, replica_groups=mesh['section'=2,'dp'=2,'seq'=8] {'dp'}, dimensions={1}, use_global_device_ids=true | all-gather | bytes 921600 | tf_op jit(solution)/shard_map/all_gather | solution.py:346
  165.8 35.8 %all-gather.4 = bf16[1,960,320]{2,0,1:T(2,128)(2,1)S(1)} all-gather(bf16[1,480,320]{2,0,1:T(2,128)(2,1)} %copy.291), channel_id=6, replica_groups=mesh['section'=2,'dp'=2,'seq'=8] {'dp'}, dimensions={1}, use_global_device_ids=true | all-gather | bytes 921600 | tf_op jit(solution)/shard_map/all_gather | solution.py:347
  249.6 34.1 %all-gather.27.cloned.1.call-done = bf16[2,1024,640]{1,0,2:T(2,128)(2,1)} async-done(((bf16[2,128,640]{1,0,2:T(2,128)(2,1)}), bf16[2,1024,640]{1,0,2:T(2,128)(2,1)}) %all-gather.27.cloned.1.call-update) | async-done | bytes 2621456 | tf_op jit(solution)/shard_map/all_gather | solution.py:218
  287.7 25.3 while.138
  355.5 61.0 %all-gather.43.cloned.1.call-done = bf16[1,960,2560]{2,1,0:T(8,128)(2,1)} async-done(((bf16[1,480,2560]{2,1,0:T(8,128)(2,1)}), bf16[1,960,2560]{2,1,0:T(8,128)(2,1)}) %all-gather.43.cloned.1.call-update) | async-done | bytes 4915216 | tf_op jit(solution)/shard_map/all_gather | solution.py:350
  423.1 59.9 %all-gather.47.cloned.1.call-done = bf16[1,2560,960]{1,2,0:T(8,128)(2,1)} async-done(((bf16[1,2560,480]{1,2,0:T(8,128)(2,1)}), bf16[1,2560,960]{1,2,0:T(8,128)(2,1)}) %all-gather.47.cloned.1.call-update) | async-done | bytes 4915216 | tf_op jit(solution)/shard_map/all_gather | solution.py:351
  660.9 22.3 while.142
  721.8 32.8 %while.144 = (s32[]{:T(128)}, f32[2,128,5,3,64]{1,4,3,2,0:T(8,128)S(1)}, bf16[2,1024,640]{1,2,0:T(8,128)(2,1)}, bf16[2,1024,640]{1,0,2:T(2,128)(2,1)}, bf16[2,10...) while((s32[]{:T(128)}, ...), condition=%wide.region_26.27_spmd.clone, body=%wide.region_25.26_spmd.clone.sunk | while | flops 1282556544 | bytes 66773772 | solution.py:184
  780.1 24.9 reduce-scatter.139.cloned.1.call-done
  849.3 33.1 %while.145 = (s32[]{:T(128)}, f32[2,128,5,3,64]{1,4,3,2,0:T(8,128)S(1)}, bf16[2,1024,640]{1,2,0:T(8,128)(2,1)}, bf16[2,1024,640]{1,0,2:T(2,128)(2,1)}, bf16[2,10...) while((s32[]{:T(128)}, ...), condition=%wide.region_31.32_spmd.clone, body=%wide.region_30.31_spmd.clone.sunk | while | flops 1282556544 | bytes 68739880 | solution.py:184
  901.9 28.7 %reduce-scatter.141.cloned.1.call-done = bf16[128,1280]{1,0:T(8,128)(2,1)} async-done(((bf16[1024,1280]{1,0:T(8,128)(2,1)}), bf16[128,1280]{1,0:T(8,128)(2,1)}) %reduce-scatter.141.cloned.1.call-update) | async-done | bytes 327696
  977.9 33.1 %while.146 = (s32[]{:T(128)}, f32[2,128,5,3,64]{1,4,3,2,0:T(8,128)S(1)}, bf16[2,1024,640]{1,2,0:T(8,128)(2,1)}, bf16[2,1024,640]{1,0,2:T(2,128)(2,1)}, bf16[2,10...) while((s32[]{:T(128)}, ...), condition=%wide.region_36.37_spmd.clone, body=%wide.region_35.36_spmd.clone.sunk | while | flops 1282556544 | bytes 68739880 | solution.py:184
  1147.4 39.5 %reduce-scatter.121.cloned.1.call-done = bf16[480,2560]{1,0:T(8,128)(2,1)} async-done(((bf16[960,2560]{1,0:T(8,128)(2,1)}), bf16[480,2560]{1,0:T(8,128)(2,1)}) %reduce-scatter.121.cloned.1.call-update) | async-done | bytes 2457616 | tf_op jit(solution)/shard_map/reduce_scatter | solution.py:396
  1191.3 59.9 %reduce-scatter.133.cloned.1.call-done = bf16[2560,480]{0,1:T(8,128)(2,1)} async-done(((bf16[2560,960]{0,1:T(8,128)(2,1)}), bf16[2560,480]{0,1:T(8,128)(2,1)}) %reduce-scatter.133.cloned.1.call-update) | async-done | bytes 2457616 | tf_op jit(solution)/shard_map/reduce_scatter | solution.py:402
  1255.6 28.1 %reduce-scatter.163.cloned.1.call-done = bf16[480,960]{1,0:T(8,128)(2,1)} async-done(((bf16[960,960]{1,0:T(8,128)(2,1)}), bf16[480,960]{1,0:T(8,128)(2,1)}) %reduce-scatter.163.cloned.1.call-update) | async-done | bytes 921616
  1286.0 30.4 %reduce-scatter.165.cloned.1.call-done = bf16[480,960]{1,0:T(8,128)(2,1)} async-done(((bf16[960,960]{1,0:T(8,128)(2,1)}), bf16[480,960]{1,0:T(8,128)(2,1)}) %reduce-scatter.165.cloned.1.call-update) | async-done | bytes 921616
  1318.8 30.2 %reduce-scatter.167.cloned.1.call-done = bf16[480,960]{1,0:T(8,128)(2,1)} async-done(((bf16[960,960]{1,0:T(8,128)(2,1)}), bf16[480,960]{1,0:T(8,128)(2,1)}) %reduce-scatter.167.cloned.1.call-update) | async-done | bytes 921616
  1467.6 62.5 %reduce-scatter.129.cloned.1.call-done = bf16[480,2560]{1,0:T(8,128)(2,1)} async-done(((bf16[960,2560]{1,0:T(8,128)(2,1)}), bf16[480,2560]{1,0:T(8,128)(2,1)}) %reduce-scatter.129.cloned.1.call-update) | async-done | bytes 2457616 | tf_op jit(solution)/shard_map/reduce_scatter | solution.py:399
  1534.5 60.2 %reduce-scatter.123.cloned.1.call-done = bf16[480,2560]{1,0:T(8,128)(2,1)} async-done(((bf16[960,2560]{1,0:T(8,128)(2,1)}), bf16[480,2560]{1,0:T(8,128)(2,1)}) %reduce-scatter.123.cloned.1.call-update) | async-done | bytes 2457616 | tf_op jit(solution)/shard_map/reduce_scatter | solution.py:396
  1599.2 28.3 %reduce-scatter.97.cloned.1.call-done = bf16[480,960]{1,0:T(8,128)(2,1)} async-done(((bf16[960,960]{1,0:T(8,128)(2,1)}), bf16[480,960]{1,0:T(8,128)(2,1)}) %reduce-scatter.97.cloned.1.call-update) | async-done | bytes 921616 | tf_op jit(solution)/shard_map/reduce_scatter | solution.py:384
  1629.8 30.2 %reduce-scatter.99.cloned.1.call-done = bf16[480,960]{1,0:T(8,128)(2,1)} async-done(((bf16[960,960]{1,0:T(8,128)(2,1)}), bf16[480,960]{1,0:T(8,128)(2,1)}) %reduce-scatter.99.cloned.1.call-update) | async-done | bytes 921616 | tf_op jit(solution)/shard_map/reduce_scatter | solution.py:384
  1662.3 30.5 %reduce-scatter.101.cloned.1.call-done = bf16[480,960]{1,0:T(8,128)(2,1)} async-done(((bf16[960,960]{1,0:T(8,128)(2,1)}), bf16[480,960]{1,0:T(8,128)(2,1)}) %reduce-scatter.101.cloned.1.call-update) | async-done | bytes 921616 | tf_op jit(solution)/shard_map/reduce_scatter | solution.py:384
  1695.1 62.2 %reduce-scatter.135.cloned.1.call-done = bf16[2560,480]{0,1:T(8,128)(2,1)} async-done(((bf16[2560,960]{0,1:T(8,128)(2,1)}), bf16[2560,480]{0,1:T(8,128)(2,1)}) %reduce-scatter.135.cloned.1.call-update) | async-done | bytes 2457616 | tf_op jit(solution)/shard_map/reduce_scatter | solution.py:402
  1761.7 59.9 %reduce-scatter.137.cloned.1.call-done = bf16[2560,480]{0,1:T(8,128)(2,1)} async-done(((bf16[2560,960]{0,1:T(8,128)(2,1)}), bf16[2560,480]{0,1:T(8,128)(2,1)}) %reduce-scatter.137.cloned.1.call-update) | async-done | bytes 2457616 | tf_op jit(solution)/shard_map/reduce_scatter | solution.py:402
  1826.0 60.1 %reduce-scatter.131.cloned.1.call-done = bf16[480,2560]{1,0:T(8,128)(2,1)} async-done(((bf16[960,2560]{1,0:T(8,128)(2,1)}), bf16[480,2560]{1,0:T(8,128)(2,1)}) %reduce-scatter.131.cloned.1.call-update) | async-done | bytes 2457616 | tf_op jit(solution)/shard_map/reduce_scatter | solution.py:399
  1890.5 60.0 %reduce-scatter.125.cloned.1.call-done = bf16[480,2560]{1,0:T(8,128)(2,1)} async-done(((bf16[960,2560]{1,0:T(8,128)(2,1)}), bf16[480,2560]{1,0:T(8,128)(2,1)}) %reduce-scatter.125.cloned.1.call-update) | async-done | bytes 2457616 | tf_op jit(solution)/shard_map/reduce_scatter | solution.py:396
  1957.8 32.4 %reduce-scatter.175.cloned.1.call-done = bf16[320,480]{1,0:T(8,128)(2,1)} async-done(((bf16[2560,480]{1,0:T(8,128)(2,1)}), bf16[320,480]{1,0:T(8,128)(2,1)}) %reduce-scatter.175.cloned.1.call-update) | async-done | bytes 307216
  1992.2 36.9 %reduce-scatter.169.cloned.1.call-done = bf16[320,480]{1,0:T(8,128)(2,1)} async-done(((bf16[2560,480]{1,0:T(8,128)(2,1)}), bf16[320,480]{1,0:T(8,128)(2,1)}) %reduce-scatter.169.cloned.1.call-update) | async-done | bytes 307216
  2031.0 37.0 %reduce-scatter.181.cloned.1.call-done = bf16[320,480]{1,0:T(8,128)(2,1)} async-done(((bf16[2560,480]{1,0:T(8,128)(2,1)}), bf16[320,480]{1,0:T(8,128)(2,1)}) %reduce-scatter.181.cloned.1.call-update) | async-done | bytes 307216
  2083.9 26.0 all-reduce.6
  2112.0 22.3 reduce-scatter.117.cloned.1.call-done
  2134.3 32.7 %reduce-scatter.119.cloned.1.call-done = bf16[120,480]{1,0:T(8,128)(2,1)} async-done(((bf16[960,480]{1,0:T(8,128)(2,1)}), bf16[120,480]{1,0:T(8,128)(2,1)}) %reduce-scatter.119.cloned.1.call-update) | async-done | bytes 115216 | tf_op jit(solution)/shard_map/reduce_scatter | solution.py:419
  2168.7 29.5 %reduce-scatter.109.cloned.1.call-done = bf16[480,40]{0,1:T(8,128)(2,1)} async-done(((bf16[480,320]{0,1:T(8,128)(2,1)}), bf16[480,40]{0,1:T(8,128)(2,1)}) %reduce-scatter.109.cloned.1.call-update) | async-done | bytes 38416 | tf_op jit(solution)/shard_map/reduce_scatter | solution.py:416
  2198.2 30.8 %reduce-scatter.111.cloned.1.call-done = bf16[480,40]{0,1:T(8,128)(2,1)} async-done(((bf16[480,320]{0,1:T(8,128)(2,1)}), bf16[480,40]{0,1:T(8,128)(2,1)}) %reduce-scatter.111.cloned.1.call-update) | async-done | bytes 38416 | tf_op jit(solution)/shard_map/reduce_scatter | solution.py:416
  2228.9 31.1 %reduce-scatter.113.cloned.1.call-done = bf16[480,40]{0,1:T(8,128)(2,1)} async-done(((bf16[480,320]{0,1:T(8,128)(2,1)}), bf16[480,40]{0,1:T(8,128)(2,1)}) %reduce-scatter.113.cloned.1.call-update) | async-done | bytes 38416 | tf_op jit(solution)/shard_map/reduce_scatter | solution.py:416
  2261.5 29.4 %reduce-scatter.103.cloned.1.call-done = bf16[480,40]{0,1:T(8,128)(2,1)} async-done(((bf16[480,320]{0,1:T(8,128)(2,1)}), bf16[480,40]{0,1:T(8,128)(2,1)}) %reduce-scatter.103.cloned.1.call-update) | async-done | bytes 38416 | tf_op jit(solution)/shard_map/reduce_scatter | solution.py:413
  2290.9 31.0 %reduce-scatter.105.cloned.1.call-done = bf16[480,40]{0,1:T(8,128)(2,1)} async-done(((bf16[480,320]{0,1:T(8,128)(2,1)}), bf16[480,40]{0,1:T(8,128)(2,1)}) %reduce-scatter.105.cloned.1.call-update) | async-done | bytes 38416 | tf_op jit(solution)/shard_map/reduce_scatter | solution.py:413
  2321.8 30.9 %reduce-scatter.107.cloned.1.call-done = bf16[480,40]{0,1:T(8,128)(2,1)} async-done(((bf16[480,320]{0,1:T(8,128)(2,1)}), bf16[480,40]{0,1:T(8,128)(2,1)}) %reduce-scatter.107.cloned.1.call-update) | async-done | bytes 38416 | tf_op jit(solution)/shard_map/reduce_scatter | solution.py:413
  2354.2 36.6 %reduce-scatter.177.cloned.1.call-done = bf16[320,480]{1,0:T(8,128)(2,1)} async-done(((bf16[2560,480]{1,0:T(8,128)(2,1)}), bf16[320,480]{1,0:T(8,128)(2,1)}) %reduce-scatter.177.cloned.1.call-update) | async-done | bytes 307216
  2391.9 37.5 %reduce-scatter.171.cloned.1.call-done = bf16[320,480]{1,0:T(8,128)(2,1)} async-done(((bf16[2560,480]{1,0:T(8,128)(2,1)}), bf16[320,480]{1,0:T(8,128)(2,1)}) %reduce-scatter.171.cloned.1.call-update) | async-done | bytes 307216
  2430.6 32.1 %reduce-scatter.145.cloned.1.call-done = bf16[120,480]{1,0:T(8,128)(2,1)} async-done(((bf16[960,480]{1,0:T(8,128)(2,1)}), bf16[120,480]{1,0:T(8,128)(2,1)}) %reduce-scatter.145.cloned.1.call-update) | async-done | bytes 115216
  2463.8 31.5 %reduce-scatter.147.cloned.1.call-done = bf16[120,480]{1,0:T(8,128)(2,1)} async-done(((bf16[960,480]{1,0:T(8,128)(2,1)}), bf16[120,480]{1,0:T(8,128)(2,1)}) %reduce-scatter.147.cloned.1.call-update) | async-done | bytes 115216
  2496.4 31.8 %reduce-scatter.149.cloned.1.call-done = bf16[120,480]{1,0:T(8,128)(2,1)} async-done(((bf16[960,480]{1,0:T(8,128)(2,1)}), bf16[120,480]{1,0:T(8,128)(2,1)}) %reduce-scatter.149.cloned.1.call-update) | async-done | bytes 115216
  2529.9 36.3 %reduce-scatter.183.cloned.1.call-done = bf16[320,480]{1,0:T(8,128)(2,1)} async-done(((bf16[2560,480]{1,0:T(8,128)(2,1)}), bf16[320,480]{1,0:T(8,128)(2,1)}) %reduce-scatter.183.cloned.1.call-update) | async-done | bytes 307216
  2567.4 37.6 %reduce-scatter.185.cloned.1.call-done = bf16[320,480]{1,0:T(8,128)(2,1)} async-done(((bf16[2560,480]{1,0:T(8,128)(2,1)}), bf16[320,480]{1,0:T(8,128)(2,1)}) %reduce-scatter.185.cloned.1.call-update) | async-done | bytes 307216
  2607.5 36.4 %reduce-scatter.179.cloned.1.call-done = bf16[320,480]{1,0:T(8,128)(2,1)} async-done(((bf16[2560,480]{1,0:T(8,128)(2,1)}), bf16[320,480]{1,0:T(8,128)(2,1)}) %reduce-scatter.179.cloned.1.call-update) | async-done | bytes 307216
  2646.3 36.5 %reduce-scatter.173.cloned.1.call-done = bf16[320,480]{1,0:T(8,128)(2,1)} async-done(((bf16[2560,480]{1,0:T(8,128)(2,1)}), bf16[320,480]{1,0:T(8,128)(2,1)}) %reduce-scatter.173.cloned.1.call-update) | async-done | bytes 307216
  (1050 shorter events, 1099.7 us)
Async XLA Ops:
  7.2 198.6 %all-gather.37.cloned.1.call-start = ((), (), s32[]{:S(2)}) async-start(), calls=%async_computation.71 | async-start | bytes 2949120 | tf_op jit(solution)/shard_map/all_gather | solution.py:339
  7.9 202.4 %all-gather.41.cloned.1.call-start = ((), (), s32[]{:S(2)}) async-start(), calls=%async_computation.73 | async-start | bytes 2949120 | tf_op jit(solution)/shard_map/all_gather | solution.py:340
  8.7 218.7 %all-gather.33.cloned.1.call-start = ((), (), s32[]{:S(2)}) async-start(), calls=%async_computation.69 | async-start | bytes 2949120 | tf_op jit(solution)/shard_map/all_gather | solution.py:345
  70.1 213.6 %all-gather.27.cloned.1.call-start = ((), (), s32[]{:S(2)}) async-start(), calls=%async_computation.45 | async-start | bytes 2949120 | tf_op jit(solution)/shard_map/all_gather | solution.py:218
  210.3 206.3 %all-gather.43.cloned.1.call-start = ((), (), s32[]{:S(2)}) async-start(), calls=%async_computation.74 | async-start | bytes 7372800 | tf_op jit(solution)/shard_map/all_gather | solution.py:350
  214.8 268.2 %all-gather.47.cloned.1.call-start = ((), (), s32[]{:S(2)}) async-start(), calls=%async_computation.76 | async-start | bytes 7372800 | tf_op jit(solution)/shard_map/all_gather | solution.py:351
  249.6 295.2 %all-gather.29.cloned.1.call-start = ((), (), s32[]{:S(2)}) async-start(), calls=%async_computation.46 | async-start | bytes 2949120 | tf_op jit(solution)/shard_map/all_gather | solution.py:218
  617.5 187.6 %reduce-scatter.139.cloned.1.call-start = ((), (), s32[]{:S(2)}) async-start(), calls=%async_computation.77 | async-start | bytes 2949120
  1033.5 217.7 %reduce-scatter.133.cloned.1.call-start = ((), (), s32[]{:S(2)}) async-start(), calls=%async_computation.66 | async-start | bytes 7372800 | tf_op jit(solution)/shard_map/reduce_scatter | solution.py:402
  1038.7 245.0 %reduce-scatter.163.cloned.1.call-start = ((), (), s32[]{:S(2)}) async-start(), calls=%async_computation.89 | async-start | bytes 2949120
  1046.4 270.1 %reduce-scatter.165.cloned.1.call-start = ((), (), s32[]{:S(2)}) async-start(), calls=%async_computation.90 | async-start | bytes 2949120
  1053.9 295.1 %reduce-scatter.167.cloned.1.call-start = ((), (), s32[]{:S(2)}) async-start(), calls=%async_computation.91 | async-start | bytes 2949120
  1061.4 306.9 %reduce-scatter.157.cloned.1.call-start = ((), (), s32[]{:S(2)}) async-start(), calls=%async_computation.86 | async-start | bytes 1105920
  1084.8 302.7 %reduce-scatter.159.cloned.1.call-start = ((), (), s32[]{:S(2)}) async-start(), calls=%async_computation.87 | async-start | bytes 1105920
  1088.5 318.4 %reduce-scatter.161.cloned.1.call-start = ((), (), s32[]{:S(2)}) async-start(), calls=%async_computation.88 | async-start | bytes 1105920
  1092.1 334.0 %reduce-scatter.151.cloned.1.call-start = ((), (), s32[]{:S(2)}) async-start(), calls=%async_computation.83 | async-start | bytes 1105920
  1095.7 350.2 %reduce-scatter.153.cloned.1.call-start = ((), (), s32[]{:S(2)}) async-start(), calls=%async_computation.84 | async-start | bytes 1105920
  1099.5 366.2 %reduce-scatter.155.cloned.1.call-start = ((), (), s32[]{:S(2)}) async-start(), calls=%async_computation.85 | async-start | bytes 1105920
  1103.0 427.1 %reduce-scatter.129.cloned.1.call-start = ((), (), s32[]{:S(2)}) async-start(), calls=%async_computation.64 | async-start | bytes 7372800 | tf_op jit(solution)/shard_map/reduce_scatter | solution.py:399
  1108.1 486.6 %reduce-scatter.123.cloned.1.call-start = ((), (), s32[]{:S(2)}) async-start(), calls=%async_computation.61 | async-start | bytes 7372800 | tf_op jit(solution)/shard_map/reduce_scatter | solution.py:396
  1113.2 514.3 %reduce-scatter.97.cloned.1.call-start = ((), (), s32[]{:S(2)}) async-start(), calls=%async_computation.48 | async-start | bytes 2949120 | tf_op jit(solution)/shard_map/reduce_scatter | solution.py:384
  1116.2 543.7 %reduce-scatter.99.cloned.1.call-start = ((), (), s32[]{:S(2)}) async-start(), calls=%async_computation.49 | async-start | bytes 2949120 | tf_op jit(solution)/shard_map/reduce_scatter | solution.py:384
  1119.4 573.4 %reduce-scatter.101.cloned.1.call-start = ((), (), s32[]{:S(2)}) async-start(), calls=%async_computation.50 | async-start | bytes 2949120 | tf_op jit(solution)/shard_map/reduce_scatter | solution.py:384
  1121.5 635.8 %reduce-scatter.135.cloned.1.call-start = ((), (), s32[]{:S(2)}) async-start(), calls=%async_computation.67 | async-start | bytes 7372800 | tf_op jit(solution)/shard_map/reduce_scatter | solution.py:402
  1126.6 695.0 %reduce-scatter.137.cloned.1.call-start = ((), (), s32[]{:S(2)}) async-start(), calls=%async_computation.68 | async-start | bytes 7372800 | tf_op jit(solution)/shard_map/reduce_scatter | solution.py:402
  1132.6 753.5 %reduce-scatter.131.cloned.1.call-start = ((), (), s32[]{:S(2)}) async-start(), calls=%async_computation.65 | async-start | bytes 7372800 | tf_op jit(solution)/shard_map/reduce_scatter | solution.py:399
  1137.5 813.1 %reduce-scatter.125.cloned.1.call-start = ((), (), s32[]{:S(2)}) async-start(), calls=%async_computation.62 | async-start | bytes 7372800 | tf_op jit(solution)/shard_map/reduce_scatter | solution.py:396
  1142.6 847.7 %reduce-scatter.175.cloned.1.call-start = ((), (), s32[]{:S(2)}) async-start(), calls=%async_computation.95 | async-start | bytes 2949120
  1147.1 882.0 %reduce-scatter.169.cloned.1.call-start = ((), (), s32[]{:S(2)}) async-start(), calls=%async_computation.92 | async-start | bytes 2949120
  1191.2 876.8 %reduce-scatter.181.cloned.1.call-start = ((), (), s32[]{:S(2)}) async-start(), calls=%async_computation.98 | async-start | bytes 2949120
  1255.6 856.4 %reduce-scatter.115.cloned.1.call-start = ((), (), s32[]{:S(2)}) async-start(), calls=%async_computation.57 | async-start | bytes 1105920 | tf_op jit(solution)/shard_map/reduce_scatter | solution.py:419
  1286.0 848.3 %reduce-scatter.117.cloned.1.call-start = ((), (), s32[]{:S(2)}) async-start(), calls=%async_computation.58 | async-start | bytes 1105920 | tf_op jit(solution)/shard_map/reduce_scatter | solution.py:419
  1318.8 848.2 %reduce-scatter.119.cloned.1.call-start = ((), (), s32[]{:S(2)}) async-start(), calls=%async_computation.59 | async-start | bytes 1105920 | tf_op jit(solution)/shard_map/reduce_scatter | solution.py:419
  1351.2 846.9 %reduce-scatter.109.cloned.1.call-start = ((), (), s32[]{:S(2)}) async-start(), calls=%async_computation.54 | async-start | bytes 368640 | tf_op jit(solution)/shard_map/reduce_scatter | solution.py:416
  1370.2 858.8 %reduce-scatter.111.cloned.1.call-start = ((), (), s32[]{:S(2)}) async-start(), calls=%async_computation.55 | async-start | bytes 368640 | tf_op jit(solution)/shard_map/reduce_scatter | solution.py:416
  1389.5 870.6 %reduce-scatter.113.cloned.1.call-start = ((), (), s32[]{:S(2)}) async-start(), calls=%async_computation.56 | async-start | bytes 368640 | tf_op jit(solution)/shard_map/reduce_scatter | solution.py:416
  1408.8 882.1 %reduce-scatter.103.cloned.1.call-start = ((), (), s32[]{:S(2)}) async-start(), calls=%async_computation.51 | async-start | bytes 368640 | tf_op jit(solution)/shard_map/reduce_scatter | solution.py:413
  1427.9 893.9 %reduce-scatter.105.cloned.1.call-start = ((), (), s32[]{:S(2)}) async-start(), calls=%async_computation.52 | async-start | bytes 368640 | tf_op jit(solution)/shard_map/reduce_scatter | solution.py:413
  1447.8 904.9 %reduce-scatter.107.cloned.1.call-start = ((), (), s32[]{:S(2)}) async-start(), calls=%async_computation.53 | async-start | bytes 368640 | tf_op jit(solution)/shard_map/reduce_scatter | solution.py:413
  1467.6 923.1 %reduce-scatter.177.cloned.1.call-start = ((), (), s32[]{:S(2)}) async-start(), calls=%async_computation.96 | async-start | bytes 2949120
  1534.5 894.9 %reduce-scatter.171.cloned.1.call-start = ((), (), s32[]{:S(2)}) async-start(), calls=%async_computation.93 | async-start | bytes 2949120
  1599.1 863.6 %reduce-scatter.145.cloned.1.call-start = ((), (), s32[]{:S(2)}) async-start(), calls=%async_computation.80 | async-start | bytes 1105920
  1629.7 865.6 %reduce-scatter.147.cloned.1.call-start = ((), (), s32[]{:S(2)}) async-start(), calls=%async_computation.81 | async-start | bytes 1105920
  1662.2 865.9 %reduce-scatter.149.cloned.1.call-start = ((), (), s32[]{:S(2)}) async-start(), calls=%async_computation.82 | async-start | bytes 1105920
  1695.0 871.1 %reduce-scatter.183.cloned.1.call-start = ((), (), s32[]{:S(2)}) async-start(), calls=%async_computation.99 | async-start | bytes 2949120
  1761.6 843.4 %reduce-scatter.185.cloned.1.call-start = ((), (), s32[]{:S(2)}) async-start(), calls=%async_computation.100 | async-start | bytes 2949120
  1826.0 817.9 %reduce-scatter.179.cloned.1.call-start = ((), (), s32[]{:S(2)}) async-start(), calls=%async_computation.97 | async-start | bytes 2949120
  1890.5 792.2 %reduce-scatter.173.cloned.1.call-start = ((), (), s32[]{:S(2)}) async-start(), calls=%async_computation.94 | async-start | bytes 2949120
  (210 other events, 5534.0 us)
Sparse Core Ops, SparseCore 0:
  9.7 45.4 all-gather.36
  56.8 36.9 all-gather.40
  95.9 41.3 all-gather.32
  138.7 70.8 all-gather.34
  211.1 33.8 all-gather.44
  246.5 37.2 all-gather.26
  285.2 64.8 all-gather.38
  351.6 64.8 all-gather.42
  418.1 64.8 all-gather.46
  507.4 37.3 all-gather.28
  617.6 39.1 all-gather.30
  766.2 38.7 reduce-scatter.138
  893.8 36.7 reduce-scatter.140
  1022.5 36.7 reduce-scatter.142
  1061.4 61.0 reduce-scatter.126
  1124.7 62.1 reduce-scatter.120
  1189.0 62.0 reduce-scatter.132
  1253.3 30.4 reduce-scatter.162
  1286.0 30.3 reduce-scatter.164
  1318.6 30.3 reduce-scatter.166
  1467.9 62.1 reduce-scatter.128
  1532.5 62.1 reduce-scatter.122
  1597.0 30.3 reduce-scatter.96
  1629.5 30.3 reduce-scatter.98
  1662.3 30.3 reduce-scatter.100
  1695.1 62.1 reduce-scatter.134
  1759.4 62.1 reduce-scatter.136
  1823.9 62.1 reduce-scatter.130
  1888.4 62.1 reduce-scatter.124
  1952.7 37.5 reduce-scatter.174
  1992.4 36.6 reduce-scatter.168
  2031.4 36.5 reduce-scatter.180
  2070.2 31.0 reduce-scatter.114
  2103.6 30.5 reduce-scatter.116
  2136.6 30.3 reduce-scatter.118
  2169.3 28.8 reduce-scatter.108
  2231.3 28.7 reduce-scatter.112
  2293.1 28.7 reduce-scatter.104
  2323.9 28.6 reduce-scatter.106
  2354.9 35.7 reduce-scatter.176
  2393.0 36.3 reduce-scatter.170
  2431.8 30.9 reduce-scatter.144
  2464.9 30.3 reduce-scatter.146
  2497.7 30.3 reduce-scatter.148
  2530.3 35.8 reduce-scatter.182
  2568.5 36.4 reduce-scatter.184
  2607.3 36.4 reduce-scatter.178
  2646.1 36.5 reduce-scatter.172
  (8 shorter events, 158.2 us)
where the time goes:
time: 2710 us; the launch traced here: 2690 us
  waiting for transfers between devices  1710 us (63%)
  local copies, waits for them, and re-layouts  311 us (11%)
  matrix products  292 us (11%)
  blocking collectives  232 us (9%)
  other arithmetic  102 us (4%)
    unnamed x80, waiting for transfers between devices  672 us
    unnamed x448, local copies, waits for them, and re-layouts  186 us
    reduce_scatter x3, waiting for transfers between devices, reduce_grads(): lax.psum_scatter(down_grad.astype(jnp.bfloat16), 'dp', scatter_dimension=...  182 us
    reduce_scatter x3, waiting for transfers between devices, reduce_grads(): lax.psum_scatter(gate_grad.astype(jnp.bfloat16), 'dp', scatter_dimension=...  160 us
    reduce_scatter x3, waiting for transfers between devices, reduce_grads(): lax.psum_scatter(up_grad.astype(jnp.bfloat16), 'dp', scatter_dimension=0,...  123 us
    reduce_scatter x3, waiting for transfers between devices, reduce_grads(): lax.psum_scatter(first[2].astype(jnp.bfloat16), 'seq', scatter_dimension=...  91.3 us
    reduce_scatter x3, waiting for transfers between devices, reduce_grads(): lax.psum_scatter(first[1].astype(jnp.bfloat16), 'seq', scatter_dimension=...  91.2 us
    reduce_scatter x3, waiting for transfers between devices, reduce_grads(): lax.psum_scatter(query_grad.astype(jnp.bfloat16), 'dp', scatter_dimension...  88.9 us
  transfers between devices with their start and end apart: 60, of which 52 were waited for; matrix products, arithmetic and copies ran while one was open for 14% of the time, Pallas kernels for 0%

commit v1 on v0

v1 whole, which is shorter than its diff:
```python
import math

import jax
import jax.numpy as jnp
from jax import lax
from jax.sharding import PartitionSpec as P

D = 960
HEADS = 15
KV_HEADS = 5
HEAD_DIM = 64
SEQ_MB = 2


EPS = 1e-05
THETA = 100000.0
MASKED = -1e30


def shifted(value, axis, steps):
    count = lax.axis_size(axis)
    leading, last = (max(0, -steps), min(count, count - steps))
    return lax.ppermute(value, axis, [(source, source + steps) for source in range(leading, last)])


def rope_tables(positions):
    half_size = HEAD_DIM // 2
    exponent = jnp.arange(half_size, dtype=jnp.float32) * (2.0 / HEAD_DIM)
    frequency = jnp.exp(-exponent * math.log(THETA))
    angles = positions.astype(jnp.float32)[..., None] * frequency
    return (jnp.cos(angles), jnp.sin(angles))


def inner_rows(left, right):
    return lax.dot_general(
        left, right, (((0,), (0,)), ((), ())), preferred_element_type=jnp.float32
    )


def against(left, weight):
    return lax.dot_general(
        left, weight, (((1,), (1,)), ((), ())), preferred_element_type=jnp.float32
    )


def normalize(values, gain):
    scale = lax.rsqrt(jnp.mean(values * values, axis=-1, keepdims=True) + EPS)
    return (scale, (values * scale * gain).astype(jnp.bfloat16))


def norm_back(gradient, values, scale, gain):
    weighted = gradient * gain
    inward = scale * weighted - values * (scale * scale * scale) * jnp.mean(
        weighted * values, axis=-1, keepdims=True
    )
    return (inward, jnp.sum(gradient * values * scale, axis=0))


def key_slice(gathered, segment_all, begin, width):
    count = gathered.shape[0]
    key_width = KV_HEADS * HEAD_DIM
    block = lax.dynamic_slice_in_dim(gathered, begin, width, 1)
    segment_block = lax.dynamic_slice_in_dim(segment_all, begin, width, 1)
    keys = block[..., :key_width].reshape(count, width, KV_HEADS, HEAD_DIM)
    values = block[..., key_width:].reshape(count, width, KV_HEADS, HEAD_DIM)
    return (keys, values, segment_block)


def masked_scores(query_view, keys, segment_block, segment_mark, query_index, begin):
    width = keys.shape[1]
    scores = jnp.einsum(
        "sqgrd,skgd->sgrqk", query_view, keys, preferred_element_type=jnp.float32
    ) * HEAD_DIM ** (-0.5)
    key_index = begin + jnp.arange(width)
    allowed = (key_index[None, None, :] <= query_index[None, :, None]) & (
        segment_block[:, None, :] == segment_mark[:, :, None]
    )
    return jnp.where(allowed[:, None, None], scores, MASKED)


def block_width():
    return 512


def attend(query_view, gathered, segment_all, segment_mark, query_index):
    count, local_length, groups, ratio, head_size = query_view.shape
    key_length = gathered.shape[1]
    width = block_width()
    blocks = key_length // width
    row_shape = (count, groups, ratio, local_length)

    def measure(index, carry):
        top, total = carry
        begin = index * width
        keys, values, segment_block = key_slice(gathered, segment_all, begin, width)
        scores = masked_scores(query_view, keys, segment_block, segment_mark, query_index, begin)
        new_top = jnp.maximum(top, jnp.max(scores, axis=-1))
        total = total * jnp.exp(top - new_top) + jnp.sum(
            jnp.exp(scores - new_top[..., None]), axis=-1
        )
        return (new_top, total)

    start = (jnp.full(row_shape, MASKED, jnp.float32), jnp.zeros(row_shape, jnp.float32))
    top, total = lax.fori_loop(0, blocks, measure, start)
    log_total = top + jnp.log(total)

    def gather_mix(index, running):
        begin = index * width
        keys, values, segment_block = key_slice(gathered, segment_all, begin, width)
        scores = masked_scores(query_view, keys, segment_block, segment_mark, query_index, begin)
        shares = jnp.exp(scores - log_total[..., None]).astype(jnp.bfloat16)
        return running + jnp.einsum(
            "sgrqk,skgd->sqgrd", shares, values, preferred_element_type=jnp.float32
        )

    mixed = lax.fori_loop(0, blocks, gather_mix, jnp.zeros(query_view.shape, jnp.float32))
    return (mixed, log_total)


def attend_back(
    query_view, gathered, segment_all, segment_mark, query_index, log_total, back_view, delta
):
    count = query_view.shape[0]
    key_length = gathered.shape[1]
    key_width = KV_HEADS * HEAD_DIM
    width = block_width()
    blocks = key_length // width
    scale = HEAD_DIM ** (-0.5)

    def sweep(index, carry):
        back_query, buffer = carry
        begin = index * width
        keys, values, segment_block = key_slice(gathered, segment_all, begin, width)
        scores = masked_scores(query_view, keys, segment_block, segment_mark, query_index, begin)
        shares = jnp.exp(scores - log_total[..., None])
        back_shares = jnp.einsum(
            "sqgrd,skgd->sgrqk", back_view, values, preferred_element_type=jnp.float32
        )
        back_scores = (shares * (back_shares - delta[..., None])).astype(jnp.bfloat16)
        back_values = jnp.einsum(
            "sgrqk,sqgrd->skgd",
            shares.astype(jnp.bfloat16),
            back_view,
            preferred_element_type=jnp.float32,
        )
        back_keys = (
            jnp.einsum(
                "sgrqk,sqgrd->skgd", back_scores, query_view, preferred_element_type=jnp.float32
            )
            * scale
        )
        back_query = (
            back_query
            + jnp.einsum("sgrqk,skgd->sqgrd", back_scores, keys, preferred_element_type=jnp.float32)
            * scale
        )
        piece = jnp.concatenate(
            [
                back_keys.reshape(count, width, key_width),
                back_values.reshape(count, width, key_width),
            ],
            axis=-1,
        )
        return (back_query, lax.dynamic_update_slice_in_dim(buffer, piece, begin, 1))

    start = (
        jnp.zeros(query_view.shape, jnp.float32),
        jnp.zeros((count, key_length, 2 * key_width), jnp.float32),
    )
    return lax.fori_loop(0, blocks, sweep, start)


def swap_halves(values):
    half = HEAD_DIM // 2
    width = values.shape[-1]
    lane = lax.broadcasted_iota(jnp.int32, values.shape, 1) % HEAD_DIM
    ahead = jnp.concatenate([values[:, half:], values[:, :half]], axis=1)
    behind = jnp.concatenate([values[:, width - half :], values[:, : width - half]], axis=1)
    return jnp.where(lane < half, ahead, behind)


def turn(values, cosine, sine):
    copies = values.shape[-1] // HEAD_DIM
    return values * jnp.tile(cosine, (1, copies)) + swap_halves(values) * jnp.tile(
        sine, (1, copies)
    )


def layer_forward(hidden, full, segment_mark, segment_all, cosine, sine, query_index):
    qkv_weight, out_weight, gate_up_weight, down_weight, gains = full
    count, local_length = segment_mark.shape
    rows = hidden.shape[0]
    key_width = KV_HEADS * HEAD_DIM
    query_width = HEADS * HEAD_DIM
    scale_front, normed = normalize(hidden, gains[0])
    qkv = against(normed, qkv_weight)
    turned = turn(qkv[:, : query_width + key_width], cosine, sine).astype(jnp.bfloat16)
    values = qkv[:, query_width + key_width :].astype(jnp.bfloat16)
    packed = jnp.concatenate([turned[:, query_width:], values], axis=-1)
    gathered = lax.all_gather(
        packed.reshape(count, local_length, 2 * key_width), "seq", axis=1, tiled=True
    )
    query_view = turned[:, :query_width].reshape(
        count, local_length, KV_HEADS, HEADS // KV_HEADS, HEAD_DIM
    )
    mixed, log_total = attend(query_view, gathered, segment_all, segment_mark, query_index)
    mixed_low = mixed.reshape(rows, query_width).astype(jnp.bfloat16)
    middle = hidden + jnp.dot(mixed_low, out_weight, preferred_element_type=jnp.float32)
    scale_back, normed_back = normalize(middle, gains[1])
    gate_up = against(normed_back, gate_up_weight)
    width = gate_up.shape[1] // 2
    gate, upward = gate_up[:, :width], gate_up[:, width:]
    product = (gate * jax.nn.sigmoid(gate) * upward).astype(jnp.bfloat16)
    output = middle + jnp.dot(product, down_weight, preferred_element_type=jnp.float32)
    kept = (
        hidden,
        scale_front,
        normed,
        query_view,
        gathered,
        mixed,
        log_total,
        mixed_low,
        middle,
        scale_back,
        normed_back,
        gate_up,
        product,
    )
    return (output, kept)


def layer_backward(incoming_low, full, kept, segment_mark, segment_all, cosine, sine, query_index):
    qkv_weight, out_weight, gate_up_weight, down_weight, gains = full
    (
        hidden,
        scale_front,
        normed,
        query_view,
        gathered,
        mixed,
        log_total,
        mixed_low,
        middle,
        scale_back,
        normed_back,
        gate_up,
        product,
    ) = kept
    rows = hidden.shape[0]
    key_width = KV_HEADS * HEAD_DIM
    query_width = HEADS * HEAD_DIM
    width = gate_up.shape[1] // 2
    gate, upward = gate_up[:, :width], gate_up[:, width:]
    incoming = incoming_low.astype(jnp.float32)
    back_product = against(incoming_low, down_weight)
    sigma = jax.nn.sigmoid(gate)
    back_gate = (back_product * upward * sigma * (1.0 + gate * (1.0 - sigma))).astype(jnp.bfloat16)
    back_up = (back_product * gate * sigma).astype(jnp.bfloat16)
    back_gate_up = jnp.concatenate([back_gate, back_up], axis=1)
    back_normed = jnp.dot(back_gate_up, gate_up_weight, preferred_element_type=jnp.float32)
    inward, gain_back_grad = norm_back(back_normed, middle, scale_back, gains[1])
    back_middle = incoming + inward
    branch = back_middle.astype(jnp.bfloat16)
    back_mixed = against(branch, out_weight).astype(jnp.bfloat16)
    back_view = back_mixed.reshape(query_view.shape)
    delta = jnp.einsum("sqgrd,sqgrd->sgrq", back_view.astype(jnp.float32), mixed)
    back_query, buffer = attend_back(
        query_view, gathered, segment_all, segment_mark, query_index, log_total, back_view, delta
    )
    summed = lax.psum_scatter(
        buffer.astype(jnp.bfloat16), "seq", scatter_dimension=1, tiled=True
    ).reshape(rows, 2 * key_width)
    back_queries = turn(back_query.reshape(rows, query_width), cosine, -sine).astype(jnp.bfloat16)
    back_keys = turn(summed[:, :key_width].astype(jnp.float32), cosine, -sine).astype(jnp.bfloat16)
    back_qkv = jnp.concatenate([back_queries, back_keys, summed[:, key_width:]], axis=1)
    back_front = jnp.dot(back_qkv, qkv_weight, preferred_element_type=jnp.float32)
    inward_front, gain_front_grad = norm_back(back_front, hidden, scale_front, gains[0])
    back_hidden = back_middle + inward_front
    gains_grad = jnp.stack([gain_front_grad, gain_back_grad])
    terms = (normed, back_qkv, mixed_low, branch, normed_back, back_gate_up, product, incoming_low)
    return (back_hidden, terms, gains_grad)


GAIN_ROWS = 16


def gather_weights(shards):
    query_part, key_part, value_part, out_part, gate_part, up_part, down_part, gain_part = shards
    seq = lax.axis_size("seq")
    dp = lax.axis_size("dp")
    lanes = query_part.shape[0]
    heights = (query_part.shape[1], key_part.shape[1], value_part.shape[1], out_part.shape[0])
    gain_block = jnp.pad(
        gain_part, ((0, GAIN_ROWS - gain_part.shape[0]), (0, lanes - gain_part.shape[1]))
    )
    front = jnp.concatenate(
        [
            jnp.concatenate([query_part, key_part, value_part], axis=1).T,
            out_part,
            gain_block,
        ],
        axis=0,
    )
    rear = jnp.concatenate([jnp.concatenate([gate_part, up_part], axis=1).T, down_part], axis=0)
    front_all = lax.all_gather(front, ("seq", "dp"), axis=0, tiled=False)
    front_all = front_all.reshape(seq, dp, front.shape[0], lanes)
    rear_all = lax.all_gather(rear, ("seq", "dp"), axis=0, tiled=False)
    rear_all = rear_all.reshape(seq, dp, rear.shape[0], lanes)

    def whole(block, begin, size):
        piece = lax.slice_in_dim(block, begin, begin + size, axis=2)
        return piece.transpose(0, 2, 1, 3).reshape(seq * size, dp * lanes)

    places = [0]
    for height in heights:
        places.append(places[-1] + height)
    qkv = jnp.concatenate([whole(front_all, places[i], heights[i]) for i in range(3)], axis=0)
    out = whole(front_all, places[3], heights[3])
    gain_width = gain_part.shape[1]
    gains = lax.slice(
        front_all, (0, 0, places[4], 0), (seq, 1, places[4] + gain_part.shape[0], gain_width)
    )
    gains = gains[:, 0].transpose(1, 0, 2).reshape(gain_part.shape[0], seq * gain_width)
    step = gate_part.shape[1]
    gate_up = jnp.concatenate([whole(rear_all, 0, step), whole(rear_all, step, step)], axis=0)
    down = whole(rear_all, 2 * step, step)
    return (qkv, out, gate_up, down, gains.astype(jnp.float32))


def split_blocks(grad, seq, dp):
    rows, columns = grad.shape
    return grad.reshape(seq, rows // seq, dp, columns // dp).transpose(0, 2, 1, 3)


def scatter_sum(blocks):
    seq, dp, rows, lanes = blocks.shape
    return lax.psum_scatter(
        blocks.reshape(seq * dp * rows, lanes), ("seq", "dp"), scatter_dimension=0, tiled=True
    )


def reduce_grads(terms, gains_grad):
    normed, back_qkv, mixed_low, branch, normed_back, back_gate_up, product, incoming = terms
    seq = lax.axis_size("seq")
    dp = lax.axis_size("dp")
    key_width = KV_HEADS * HEAD_DIM
    query_width = HEADS * HEAD_DIM

    def outer(left, right):
        return inner_rows(left, right).astype(jnp.bfloat16)

    gate_up = outer(back_gate_up, normed_back)
    down = outer(product, incoming)
    hidden_width = down.shape[0]
    rear = jnp.concatenate(
        [
            split_blocks(gate_up[:hidden_width], seq, dp),
            split_blocks(gate_up[hidden_width:], seq, dp),
            split_blocks(down, seq, dp),
        ],
        axis=2,
    )
    rear = scatter_sum(rear).astype(jnp.float32)
    qkv = outer(back_qkv, normed)
    out = outer(mixed_low, branch)
    gain_kinds, gain_all = gains_grad.shape
    gain_width = gain_all // seq
    lanes = out.shape[1] // dp
    gain_block = gains_grad.astype(jnp.bfloat16).reshape(gain_kinds, seq, gain_width)
    gain_block = gain_block.transpose(1, 0, 2)
    gain_block = jnp.pad(
        gain_block, ((0, 0), (0, GAIN_ROWS - gain_kinds), (0, lanes - gain_width))
    )
    gain_block = jnp.broadcast_to(gain_block[:, None], (seq, dp, GAIN_ROWS, lanes))
    front = jnp.concatenate(
        [
            split_blocks(qkv[:query_width], seq, dp),
            split_blocks(qkv[query_width : query_width + key_width], seq, dp),
            split_blocks(qkv[query_width + key_width :], seq, dp),
            split_blocks(out, seq, dp),
            gain_block,
        ],
        axis=2,
    )
    front = scatter_sum(front).astype(jnp.float32)
    query_rows = query_width // seq
    key_rows = key_width // seq
    first = query_rows + key_rows
    second = first + key_rows
    third = second + query_rows
    hidden_rows = hidden_width // seq
    return (
        front[:query_rows].T,
        front[query_rows:first].T,
        front[first:second].T,
        front[second:third],
        rear[:hidden_rows].T,
        rear[hidden_rows : 2 * hidden_rows].T,
        rear[2 * hidden_rows :],
        front[third : third + gain_kinds, :gain_width],
    )


def pick_section(section, early, late):

    def select(early_part, late_part):
        return jnp.where(section == 0, early_part, late_part)

    return jax.tree.map(select, early, late)


def on_device(
    ends,
    segments,
    positions,
    query_weights,
    key_weights,
    value_weights,
    out_weights,
    gate_weights,
    up_weights,
    down_weights,
    norm_gains,
):
    section = lax.axis_index("section")
    sections = lax.axis_size("section")
    count = SEQ_MB
    micro = segments.shape[0] // count
    local_length = segments.shape[1]
    rows = count * local_length
    ticks = micro + sections - 1
    query_index = lax.axis_index("seq") * local_length + jnp.arange(local_length)
    shards = (
        query_weights[0],
        key_weights[0],
        value_weights[0],
        out_weights[0],
        gate_weights[0],
        up_weights[0],
        down_weights[0],
        norm_gains[0],
    )
    full = gather_weights(shards)
    outside = ends[0].reshape(micro, rows, D)
    blank = jnp.zeros((rows, D), jnp.bfloat16)

    marks = segments.astype(jnp.bfloat16)
    marks_all = lax.all_gather(marks, "seq", axis=1, tiled=True)
    cosines, sines = rope_tables(positions.reshape(micro * rows))
    cosines = jnp.concatenate([cosines, cosines], axis=1)
    sines = jnp.concatenate([-sines, sines], axis=1)

    def batch_inputs(index):
        mark = lax.dynamic_slice_in_dim(marks, index * count, count, 0)
        mark_all = lax.dynamic_slice_in_dim(marks_all, index * count, count, 0)
        cosine = lax.dynamic_slice_in_dim(cosines, index * rows, rows, 0)
        sine = lax.dynamic_slice_in_dim(sines, index * rows, rows, 0)
        return (mark, mark_all, cosine, sine)

    received = blank
    results = []
    stores = []
    for tick in range(ticks):
        own = outside[tick] if tick < micro else blank
        source = jnp.where(section == 0, own, received)
        index = jnp.clip(tick - section, 0, micro - 1)
        mark, mark_all, cosine, sine = batch_inputs(index)
        output, kept = layer_forward(
            source.astype(jnp.float32), full, mark, mark_all, cosine, sine, query_index
        )
        sent = output.astype(jnp.bfloat16)
        results.append(sent)
        stores.append(kept)
        if tick + 1 < ticks:
            received = shifted(sent, "section", 1)
    received = blank
    sent_back = []
    collected = []
    gains_grad = 0.0
    for tick in range(ticks):
        own = outside[tick] if tick < micro else blank
        incoming = jnp.where(section == sections - 1, own, received)
        index = jnp.clip(tick - 1 + section, 0, micro - 1)
        mark, mark_all, cosine, sine = batch_inputs(index)
        kept = pick_section(section, stores[max(tick - 1, 0)], stores[min(tick + 1, ticks - 1)])
        back_hidden, terms, gains_part = layer_backward(
            incoming, full, kept, mark, mark_all, cosine, sine, query_index
        )
        collected.append(terms)
        gains_grad = gains_grad + gains_part
        sent = back_hidden.astype(jnp.bfloat16)
        sent_back.append(sent)
        if tick + 1 < ticks:
            received = shifted(sent, "section", -1)
    terms = tuple(jnp.concatenate(parts, axis=0) for parts in zip(*collected))
    totals = reduce_grads(terms, gains_grad)
    outputs_list = []
    grads_list = []
    for batch in range(micro):
        outputs_list.append(
            jnp.where(section == 0, results[batch], results[batch + 1]).reshape(
                count, local_length, D
            )
        )
        grads_list.append(
            jnp.where(section == 0, sent_back[batch + 1], sent_back[batch]).reshape(
                count, local_length, D
            )
        )
    activations = jnp.concatenate(outputs_list, axis=0)[None]
    input_grads = jnp.concatenate(grads_list, axis=0)[None]
    return (
        activations,
        input_grads,
        totals[0][None],
        totals[1][None],
        totals[2][None],
        totals[3][None],
        totals[4][None],
        totals[5][None],
        totals[6][None],
        totals[7][None],
    )


def solution(mesh):
    return jax.shard_map(
        on_device,
        mesh=mesh,
        in_specs=(
            P("section", "dp", "seq", None),
            P("dp", "seq"),
            P("dp", "seq"),
            P("section", "dp", "seq"),
            P("section", "dp", "seq"),
            P("section", "dp", "seq"),
            P("section", "seq", "dp"),
            P("section", "dp", "seq"),
            P("section", "dp", "seq"),
            P("section", "seq", "dp"),
            P("section", None, "seq"),
        ),
        out_specs=(
            P("section", "dp", "seq", None),
            P("section", "dp", "seq", None),
            P("section", "dp", "seq"),
            P("section", "dp", "seq"),
            P("section", "dp", "seq"),
            P("section", "seq", "dp"),
            P("section", "dp", "seq"),
            P("section", "dp", "seq"),
            P("section", "seq", "dp"),
            P("section", None, "seq"),
        ),
        check_vma=False,
    )
```

time: 2710 us -> 1270 us (0.47)
  waiting for transfers between devices: 1710 us -> 458 us
  blocking collectives: 232 us -> 10.6 us
    unnamed x80 -> x10, waiting for transfers between devices: 672 us -> 0.16 us
    reduce_scatter x21 -> x5, waiting for transfers between devices: 791 us -> 207 us  [the longest x2 144 us: scatter_sum(): lax.psum_scatter(blocks.reshape(seq * dp * rows, lanes), ('seq', 'dp'), s...]
    all_gather x10 -> x1, blocking collectives: 198 us -> 10.6 us  [on_device(): marks_all = lax.all_gather(marks, 'seq', axis=1, tiled=True)]
    unnamed x448 -> x422, local copies, waits for them, and re-layouts: 186 us -> 44.6 us
    reshape x12 -> x23, local copies, waits for them, and re-layouts: 14.1 us -> 132 us  [the longest x11 82.3 us: split_blocks(): grad.reshape(seq, rows // seq, dp, columns // dp).transpose(0, 2, 1, 3)]
    transpose x0 -> x8, local copies, waits for them, and re-layouts: none -> 44.2 us  [the longest x7 43.4 us: whole(): return piece.transpose(0, 2, 1, 3).reshape(seq * size, dp * lanes)]
    all_gather x10 -> x0, local copies, waits for them, and re-layouts: 38.5 us -> none  [the longest x1 9.16 us: gather_weights(): lax.all_gather(wide[3], 'dp', axis=1, tiled=True)]
    dot_general x21 -> x4, matrix products: 66.3 us -> 29.9 us  [inner_rows(): lax.dot_general(left, right, (((0,), (0,)), ((), ())), preferred_element_...]
  transfers between devices with their start and end apart: 60 -> 14, of which waited for: 52 -> 12; matrix products, arithmetic and copies ran while one was open for 14% -> 19% of each run, Pallas kernels for 0% -> 0%
where the time goes in v1:
time: 1270 us; the launch traced here: 1260 us
  waiting for transfers between devices  458 us (36%)
  local copies, waits for them, and re-layouts  332 us (26%)
  matrix products  297 us (23%)
  other arithmetic  127 us (10%)
  between operations  17.7 us (1%)
    reduce_scatter x2, waiting for transfers between devices, scatter_sum(): lax.psum_scatter(blocks.reshape(seq * dp * rows, lanes), ('seq', 'dp'), s...  144 us
    all_gather x1, waiting for transfers between devices, gather_weights(): rear_all = lax.all_gather(rear, ('seq', 'dp'), axis=0, tiled=False)  83.4 us
    reshape x11, local copies, waits for them, and re-layouts, split_blocks(): grad.reshape(seq, rows // seq, dp, columns // dp).transpose(0, 2, 1, 3)  82.3 us
    all_gather x3, waiting for transfers between devices, layer_forward(): lax.all_gather(packed.reshape(count, local_length, 2 * key_width), 'seq',...  75.2 us
    reduce_scatter x3, waiting for transfers between devices, layer_backward(): lax.psum_scatter(buffer.astype(jnp.bfloat16), 'seq', scatter_dimension=1,...  63 us
    dot_general x12, matrix products, against(): lax.dot_general(left, weight, (((1,), (1,)), ((), ())), preferred_element...  59.4 us
    all_gather x1, waiting for transfers between devices, gather_weights(): front_all = lax.all_gather(front, ('seq', 'dp'), axis=0, tiled=False)  55 us
    reshape x9, local copies, waits for them, and re-layouts, whole(): return piece.transpose(0, 2, 1, 3).reshape(seq * size, dp * lanes)  48.5 us
  transfers between devices with their start and end apart: 14, of which 12 were waited for; matrix products, arithmetic and copies ran while one was open for 19% of the time, Pallas kernels for 0%

profile of v1, /device:TPU:0, one launch (start us, length us, event | category | flops | bytes accessed | tf_op | source)
XLA Modules:
  0.0 1256.0 jit_solution(233930898896547446)
XLA Ops:
  16.0 55.0 %all-gather.14.cloned.1.call-done = bf16[5376,480]{1,0:T(8,128)(2,1)} async-done(((bf16[336,480]{1,0:T(8,128)(2,1)}), bf16[5376,480]{1,0:T(8,128)(2,1)}) %all-gather.14.cloned.1.call-update) | async-done | bytes 5160976 | tf_op jit(solution)/shard_map/all_gather | solution.py:306
  112.4 10.6 all_gather.27
  133.3 11.3 all-gather.8.cloned.1.call-done
  144.6 22.3 %while.138 = (s32[]{:T(128)}, f32[2,5,3,128]{3,2,1,0:T(4,128)S(1)}, f32[2,5,3,128]{3,2,1,0:T(4,128)S(1)}, bf16[2,1024]{1,0:T(2,128)(2,1)S(1)}, bf16[2,128]{1,0:T...) while((s32[]{:T(128)}, f32[2,5,3,128]{3,2,1,0:T(4,128)S(1)}, ...), condition=%wide.region_4.5_spmd.clone, body=%wide.region_1.4_spmd.clone.sunk | while | flops 266030464 | bytes 18922180 | solution.py:104
  167.5 13.1 %while.139 = (s32[]{:T(128)}, f32[2,128,5,3,64]{1,4,3,2,0:T(8,128)S(1)}, bf16[2,1024,640]{1,2,0:T(8,128)(2,1)}, bf16[2,1024]{1,0:T(2,128)(2,1)S(1)}, bf16[2,128]...) while((s32[]{:T(128)}, ...), condition=%wide.region_6.7_spmd.clone, body=%wide.region_5.6_spmd.clone.sunk | while | flops 512262784 | bytes 6812409 | solution.py:116
  183.5 83.4 %all-gather.16.cloned.1.call-done = bf16[15360,480]{1,0:T(8,128)(2,1)} async-done(((bf16[960,480]{1,0:T(8,128)(2,1)}), bf16[15360,480]{1,0:T(8,128)(2,1)}) %all-gather.16.cloned.1.call-update) | async-done | bytes 14745616 | tf_op jit(solution)/shard_map/all_gather | solution.py:308
  266.9 8.8 fusion.312
  275.7 25.4 %copy_bitcast_fusion = (bf16[8,320,2,480]{3,2,1,0:T(2,128)(2,1)}, bf16[8,320,2,480]{3,2,1,0:T(2,128)(2,1)}) fusion(bf16[8,2,320,480]{3,2,1,0:T(8,128)(2,1)S(1)} %get-tuple-element.2196, bf16[8,2,320,480]{3,2,1,0:T(8,128)(2,1)S(1)} %get-tuple-element.2197), kind=kLoop, calls=%fused_computation.188 | loop fusion | bytes 19660800 | tf_op jit(solution)/shard_map/transpose | solution.py:313
  301.1 10.0 reshape.972
  311.0 10.2 copy.420
  321.3 9.9 reshape.970
  336.5 9.9 reshape.971
  352.0 6.4 fusion.341
  365.2 10.3 collective-permute-done
  379.9 33.9 %all-gather.10.cloned.1.call-done = bf16[2,1024,640]{1,2,0:T(8,128)(2,1)} async-done(((bf16[2,128,640]{1,2,0:T(8,128)(2,1)}), bf16[2,1024,640]{1,2,0:T(8,128)(2,1)}) %all-gather.10.cloned.1.call-update) | async-done | bytes 2621456 | tf_op jit(solution)/shard_map/all_gather | solution.py:200
  413.8 21.9 %while.140 = (s32[]{:T(128)}, f32[2,5,3,128]{3,2,1,0:T(4,128)S(1)}, f32[2,5,3,128]{3,2,1,0:T(4,128)S(1)}, bf16[2,1024]{1,0:T(2,128)(2,1)S(1)}, bf16[2,128]{1,0:T...) while((s32[]{:T(128)}, f32[2,5,3,128]{3,2,1,0:T(4,128)S(1)}, ...), condition=%wide.region_12.13_spmd.clone, body=%wide.region_9.12_spmd.clone.sunk | while | flops 266030464 | bytes 18922180 | solution.py:104
  435.8 11.6 while.141
  470.5 10.9 collective-permute-done.1
  490.8 30.0 %all-gather.12.cloned.1.call-done = bf16[2,1024,640]{1,2,0:T(8,128)(2,1)} async-done(((bf16[2,128,640]{1,2,0:T(8,128)(2,1)}), bf16[2,1024,640]{1,2,0:T(8,128)(2,1)}) %all-gather.12.cloned.1.call-update) | async-done | bytes 2621456 | tf_op jit(solution)/shard_map/all_gather | solution.py:200
  520.8 22.2 %while.142 = (s32[]{:T(128)}, f32[2,5,3,128]{3,2,1,0:T(4,128)S(1)}, f32[2,5,3,128]{3,2,1,0:T(4,128)S(1)}, bf16[2,1024]{1,0:T(2,128)(2,1)S(1)}, bf16[2,128]{1,0:T...) while((s32[]{:T(128)}, f32[2,5,3,128]{3,2,1,0:T(4,128)S(1)}, ...), condition=%wide.region_20.21_spmd.clone, body=%wide.region_17.20_spmd.clone.sunk | while | flops 266030464 | bytes 18922180 | solution.py:104
  543.6 14.7 %while.143 = (s32[]{:T(128)}, f32[2,128,5,3,64]{1,4,3,2,0:T(8,128)}, bf16[2,1024,640]{1,2,0:T(8,128)(2,1)}, bf16[2,1024]{1,0:T(2,128)(2,1)S(1)}, bf16[2,128]{1,0...) while((s32[]{:T(128)}, f32[2,128,5,3,64]{1,4,3,2,0:T(8,128)}, ...), condition=%wide.region_22.23_spmd.clone, body=%wide.region_21.22_spmd.clone.sunk | while | flops 512262784 | bytes 6810333 | solution.py:116
  563.6 13.6 %broadcast_select_fusion.3 = (f32[256,5120]{1,0:T(8,128)}, f32[256,5120]{1,0:T(8,128)}, f32[256,5120]{1,0:T(8,128)}, f32[256,5120]{1,0:T(8,128)}) fusion(f32[256,5120]{1,0:T(8,128)} %copy-done.18, pred[]{:T(512)S(6)} %eq.362, f32[256,5120]{1,0:T(8,128)} %copy-done.11, bf16[256,960]{0,1:T(8,128)(2,1)S(1)} %get-tuple-element.2146, ...), kind=kOutput, calls=%fused_computation.236 | convolution fusion | flops 2520514560 | bytes 41779200 | tf_op jit(solution)/shard_map/dot_general | solution.py:41
  577.2 6.5 fusion.135
  583.7 9.9 multiply_reduce_fusion.7
  609.7 42.6 %while.144 = (s32[]{:T(128)}, f32[2,128,5,3,64]{1,4,3,2,0:T(8,128)}, bf16[2,1024,640]{2,1,0:T(8,128)(2,1)}, bf16[2,1024,640]{1,2,0:T(8,128)(2,1)}, bf16[2,1024]{...) while((s32[]{:T(128)}, f32[2,128,5,3,64]{1,4,3,2,0:T(8,128)}, ...), condition=%wide.region_26.27_spmd.clone, body=%wide.region_25.26_spmd.clone.sunk | while | flops 1282556544 | bytes 100852536 | solution.py:170
  655.8 32.7 %reduce-scatter.6.cloned.1.call-done = bf16[2,128,640]{2,1,0:T(8,128)(2,1)} async-done(((bf16[2,1024,640]{2,1,0:T(8,128)(2,1)}), bf16[2,128,640]{2,1,0:T(8,128)(2,1)}) %reduce-scatter.6.cloned.1.call-update) | async-done | bytes 327696 | tf_op jit(solution)/shard_map/reduce_scatter | solution.py:271
  697.3 10.7 collective-permute-done.2
  709.2 8.2 fusion.132
  717.4 8.0 multiply_reduce_fusion.5
  732.6 42.5 %while.145 = (s32[]{:T(128)}, f32[2,128,5,3,64]{1,4,3,2,0:T(8,128)}, bf16[2,1024,640]{2,1,0:T(8,128)(2,1)}, bf16[2,1024,640]{1,2,0:T(8,128)(2,1)}, bf16[2,1024]{...) while((s32[]{:T(128)}, f32[2,128,5,3,64]{1,4,3,2,0:T(8,128)}, ...), condition=%wide.region_31.32_spmd.clone, body=%wide.region_30.31_spmd.clone.sunk | while | flops 1282556544 | bytes 100852536 | solution.py:170
  781.8 30.2 %reduce-scatter.8.cloned.1.call-done = bf16[2,128,640]{2,1,0:T(8,128)(2,1)} async-done(((bf16[2,1024,640]{2,1,0:T(8,128)(2,1)}), bf16[2,128,640]{2,1,0:T(8,128)(2,1)}) %reduce-scatter.8.cloned.1.call-update) | async-done | bytes 327696 | tf_op jit(solution)/shard_map/reduce_scatter | solution.py:271
  826.4 6.0 collective-permute-done.3
  832.5 8.3 fusion.129
  840.9 8.1 multiply_reduce_fusion.3
  856.6 42.8 %while.146 = (s32[]{:T(128)}, f32[2,128,5,3,64]{1,4,3,2,0:T(8,128)}, bf16[2,1024,640]{2,1,0:T(8,128)(2,1)}, bf16[2,1024,640]{1,2,0:T(8,128)(2,1)}, bf16[2,1024]{...) while((s32[]{:T(128)}, f32[2,128,5,3,64]{1,4,3,2,0:T(8,128)}, ...), condition=%wide.region_36.37_spmd.clone, body=%wide.region_35.36_spmd.clone.sunk | while | flops 1282556544 | bytes 100852536 | solution.py:170
  915.3 7.3 reshape.993
  923.2 8.4 convolution_convert_fusion.1
  931.6 9.9 reshape.1058
  941.6 11.6 copy.280
  955.3 14.2 %convolution_convert_fusion = bf16[5120,960]{0,1:T(8,128)(2,1)} fusion(bf16[256,2560]{1,0:T(8,128)(2,1)} %get-tuple-element.2202, bf16[256,2560]{1,0:T(8,128)(2,1)} %get-tuple-element.2201, bf16[256,2560]{1,0:T(8,128)(2,1)} %get-tuple-element.2204, bf16[256,2560]{1,0:T(8,128)(2,1)} %get-tuple-element.2203, bf16[256,2560]{1,0:T(8,128)(2,1)} %copy-done.194, ...), kind=kOutput, calls=%fused_computation.175 | convolution fusion | flops 7606272000 | bytes 19169280 | tf_op jit(solution)/shard_map/dot_general | solution.py:35
  1002.2 8.3 fusion.313
  1010.5 10.2 reshape.1057
  1020.6 11.7 copy.279
  1032.3 9.9 reshape.1056
  1042.2 11.7 copy.278
  1053.9 28.0 %pad_maximum_fusion.3 = bf16[8,2,960,480]{3,1,2,0:T(2,128)(2,1)S(1)} fusion(bf16[8,2,320,480]{3,1,2,0:T(2,128)(2,1)} %bitcast.875, bf16[8,2,320,480]{3,1,2,0:T(2,128)(2,1)} %bitcast.876, bf16[8,2,320,480]{3,1,2,0:T(2,128)(2,1)} %bitcast.877), kind=kLoop, calls=%fused_computation.174 | loop fusion | flops 14745600 | bytes 29491200 | tf_op jit(solution)/shard_map/concatenate | solution.py:356
  1082.0 7.2 copy.226
  1102.4 143.5 %reduce-scatter.14.cloned.1.call-done = bf16[960,480]{1,0:T(8,128)(2,1)} async-done(((bf16[15360,480]{1,0:T(8,128)(2,1)}), bf16[960,480]{1,0:T(8,128)(2,1)}) %reduce-scatter.14.cloned.1.call-update) | async-done | bytes 921616 | tf_op jit(solution)/shard_map/reduce_scatter | solution.py:338
  (877 shorter events, 485.4 us)
Async XLA Ops:
  7.2 63.8 %all-gather.14.cloned.1.call-start = ((), (), s32[]{:S(2)}) async-start(), calls=%async_computation.13 | async-start | bytes 5849088 | tf_op jit(solution)/shard_map/all_gather | solution.py:306
  10.8 133.9 %all-gather.8.cloned.1.call-start = ((), (), s32[]{:S(2)}) async-start(), calls=%async_computation.5 | async-start | bytes 2949120 | tf_op jit(solution)/shard_map/all_gather | solution.py:200
  14.0 167.2 %copy-start.12 = (f32[1,2,128,960]{2,1,3,0:T(2,128)}, f32[1,2,128,960]{2,1,3,0:T(2,128)S(1)}, u32[]{:S(2)}) copy-start(f32[1,2,128,960]{2,1,3,0:T(2,128)S(1)} %copy.162) | copy-start | bytes 2949124
  14.0 95.5 %copy-start.146 = (pred[1280]{0:T(1024)(128)(4,1)}, pred[1280]{0:T(1024)(128)(4,1)S(1)}, u32[]{:S(2)}) copy-start(pred[1280]{0:T(1024)(128)(4,1)S(1)} %fusion.282) | copy-start | bytes 3844
  14.0 95.5 %copy-start.133 = (s32[1280]{0:T(1024)}, s32[1280]{0:T(1024)S(1)}, u32[]{:S(2)}) copy-start(s32[1280]{0:T(1024)S(1)} %get-tuple-element.2330) | copy-start | bytes 15364
  16.0 58.8 %copy-start.167 = (f32[2,128]{1,0:T(2,128)}, f32[2,128]{1,0:T(2,128)S(1)}, u32[]{:S(2)}) copy-start(f32[2,128]{1,0:T(2,128)S(1)} %multiply_reduce_fusion.18) | copy-start | bytes 3076
  16.0 89.8 %copy-start.173 = (f32[256]{0:T(256)}, f32[256]{0:T(256)S(1)}, u32[]{:S(2)}) copy-start(f32[256]{0:T(256)S(1)} %rsqrt_bitcast_fusion) | copy-start | bytes 3076
  99.9 382.3 %copy-start.136 = (f32[960]{0:T(1024)}, f32[960]{0:T(1024)S(1)}, u32[]{:S(2)}) copy-start(f32[960]{0:T(1024)S(1)} %mul.927) | copy-start | bytes 11524
  111.0 155.9 %all-gather.16.cloned.1.call-start = ((), (), s32[]{:S(2)}) async-start(), calls=%async_computation.14 | async-start | bytes 16711680 | tf_op jit(solution)/shard_map/all_gather | solution.py:308
  112.2 301.6 %all-gather.10.cloned.1.call-start = ((), (), s32[]{:S(2)}) async-start(), calls=%async_computation.6 | async-start | bytes 2949120 | tf_op jit(solution)/shard_map/all_gather | solution.py:200
  133.3 715.6 %copy-start.114 = (f32[960]{0:T(1024)}, f32[960]{0:T(1024)S(1)}, u32[]{:S(2)}) copy-start(f32[960]{0:T(1024)S(1)} %mul.945) | copy-start | bytes 11524
  180.6 255.2 %copy-start.121 = (f32[2,5,3,128]{3,2,1,0:T(4,128)}, f32[2,5,3,128]{3,2,1,0:T(4,128)S(1)}, u32[]{:S(2)}) copy-start(f32[2,5,3,128]{3,2,1,0:T(4,128)S(1)} %get-tuple-element.3292) | copy-start | bytes 46084
  180.6 377.7 %copy-start.16 = (f32[2,128,5,3,64]{1,4,3,2,0:T(8,128)}, f32[2,128,5,3,64]{1,4,3,2,0:T(8,128)S(1)}, u32[]{:S(2)}) copy-start(f32[2,128,5,3,64]{1,4,3,2,0:T(8,128)S(1)} %get-tuple-element.1404) | copy-start | bytes 2949124
  183.4 92.2 %copy-start.169 = (f32[256]{0:T(256)}, f32[256]{0:T(256)S(1)}, u32[]{:S(2)}) copy-start(f32[256]{0:T(256)S(1)} %get-tuple-element.2316) | copy-start | bytes 3076
  183.5 174.9 %copy-start.25 = (f32[256,960]{0,1:T(8,128)}, f32[256,960]{0,1:T(8,128)S(1)}, u32[]{:S(2)}) copy-start(f32[256,960]{0,1:T(8,128)S(1)} %get-tuple-element.2317) | copy-start | bytes 2949124
  183.5 168.5 %copy-start.159 = (f32[256]{0:T(256)}, f32[256]{0:T(256)S(1)}, u32[]{:S(2)}) copy-start(f32[256]{0:T(256)S(1)} %add_rsqrt_fusion.4) | copy-start | bytes 3076
  358.4 17.3 %copy-start.19 = (bf16[1600,960]{0,1:T(8,128)(2,1)S(1)}, bf16[1600,960]{0,1:T(8,128)(2,1)}, u32[]{:S(2)}) copy-start(bf16[1600,960]{0,1:T(8,128)(2,1)} %concatenate.167) | copy-start | bytes 9216004
  361.1 14.4 %collective-permute-start = (bf16[256,960]{0,1:T(8,128)(2,1)S(1)}, bf16[256,960]{0,1:T(8,128)(2,1)S(1)}, u32[]{:S(2)}, u32[]{:S(2)}) collective-permute-start(bf16[256,960]{0,1:T(8,128)(2,1)S(1)} %fusion.202), channel_id=1, source_target_pairs={{0,16},{1,17},{2,18},{3,19},{4,20},{5,21},{6,22},{7,23},{8,24},{9,... | collective-permute-start | bytes 1474568 | tf_op jit(solution)/shard_map/ppermute | solution.py:23
  378.8 35.0 %copy-start.140 = (bf16[2,128]{1,0:T(2,128)(2,1)S(1)}, bf16[2,128]{1,0:T(2,128)(2,1)}, u32[]{:S(2)}) copy-start(bf16[2,128]{1,0:T(2,128)(2,1)} %get-tuple-element.2983) | copy-start | bytes 1540
  379.6 141.2 %all-gather.12.cloned.1.call-start = ((), (), s32[]{:S(2)}) async-start(), calls=%async_computation.7 | async-start | bytes 2949120 | tf_op jit(solution)/shard_map/all_gather | solution.py:200
  379.8 34.0 %copy-start.56 = (bf16[2,128,5,3,64]{1,0,4,3,2:T(2,128)(2,1)}, bf16[2,128,5,3,64]{1,0,4,3,2:T(2,128)(2,1)S(1)}, u32[]{:S(2)}) copy-start(bf16[2,128,5,3,64]{1,0,4,3,2:T(2,128)(2,1)S(1)} %reshape.974) | copy-start | bytes 1474564
  461.9 19.7 %copy-start.168 = (f32[2,128]{1,0:T(2,128)S(1)}, f32[2,128]{1,0:T(2,128)}, u32[]{:S(2)}) copy-start(f32[2,128]{1,0:T(2,128)} %copy-done.167) | copy-start | bytes 3076
  461.9 19.7 %copy-start.172 = (f32[256]{0:T(256)S(1)}, f32[256]{0:T(256)}, u32[]{:S(2)}) copy-start(f32[256]{0:T(256)} %copy-done.171) | copy-start | bytes 3076
  461.9 20.3 %copy-start.20 = (bf16[1600,960]{0,1:T(8,128)(2,1)S(1)}, bf16[1600,960]{0,1:T(8,128)(2,1)}, u32[]{:S(2)}) copy-start(bf16[1600,960]{0,1:T(8,128)(2,1)} %concatenate.167) | copy-start | bytes 9216004
  467.1 14.3 %collective-permute-start.1 = (bf16[256,960]{0,1:T(8,128)(2,1)S(1)}, bf16[256,960]{0,1:T(8,128)(2,1)S(1)}, u32[]{:S(2)}, u32[]{:S(2)}) collective-permute-start(bf16[256,960]{0,1:T(8,128)(2,1)S(1)} %fusion.203), channel_id=1, source_target_pairs={{0,16},{1,17},{2,18},{3,19},{4,20},{5,21},{6,22},{7,23},{8,24},{9,... | collective-permute-start | bytes 1474568 | tf_op jit(solution)/shard_map/ppermute | solution.py:23
  486.2 202.3 %reduce-scatter.6.cloned.1.call-start = ((), (), s32[]{:S(2)}) async-start(), calls=%async_computation.8 | async-start | bytes 2949120 | tf_op jit(solution)/shard_map/reduce_scatter | solution.py:271
  487.6 33.1 %copy-start.132 = (bf16[2,1024]{1,0:T(2,128)(2,1)S(1)}, bf16[2,1024]{1,0:T(2,128)(2,1)}, u32[]{:S(2)}) copy-start(bf16[2,1024]{1,0:T(2,128)(2,1)} %get-tuple-element.3057) | copy-start | bytes 12292
  487.6 33.1 %copy-start.139 = (bf16[2,128]{1,0:T(2,128)(2,1)S(1)}, bf16[2,128]{1,0:T(2,128)(2,1)}, u32[]{:S(2)}) copy-start(bf16[2,128]{1,0:T(2,128)(2,1)} %get-tuple-element.3058) | copy-start | bytes 1540
  652.3 159.7 %reduce-scatter.8.cloned.1.call-start = ((), (), s32[]{:S(2)}) async-start(), calls=%async_computation.9 | async-start | bytes 2949120 | tf_op jit(solution)/shard_map/reduce_scatter | solution.py:271
  652.4 161.1 %copy-start.175 = (pred[320]{0:T(512)(128)(4,1)}, pred[320]{0:T(512)(128)(4,1)S(1)}, u32[]{:S(2)}) copy-start(pred[320]{0:T(512)(128)(4,1)S(1)} %fusion.291) | copy-start | bytes 964
  652.4 161.1 %copy-start.148 = (s32[320]{0:T(512)}, s32[320]{0:T(512)S(1)}, u32[]{:S(2)}) copy-start(s32[320]{0:T(512)S(1)} %get-tuple-element.2333) | copy-start | bytes 3844
  652.4 161.1 %copy-start.149 = (s32[320]{0:T(512)}, s32[320]{0:T(512)S(1)}, u32[]{:S(2)}) copy-start(s32[320]{0:T(512)S(1)} %get-tuple-element.2334) | copy-start | bytes 3844
  655.7 38.4 %copy-start.101 = (bf16[256,960]{0,1:T(8,128)(2,1)}, bf16[256,960]{0,1:T(8,128)(2,1)S(1)}, u32[]{:S(2)}) copy-start(bf16[256,960]{0,1:T(8,128)(2,1)S(1)} %fusion.217) | copy-start | bytes 1474564
  655.8 34.5 %copy-start.13 = (f32[1,2,128,960]{2,1,3,0:T(2,128)S(1)}, f32[1,2,128,960]{2,1,3,0:T(2,128)}, u32[]{:S(2)}) copy-start(f32[1,2,128,960]{2,1,3,0:T(2,128)} %copy-done.12) | copy-start | bytes 2949124
  655.8 34.5 %copy-start.49 = (bf16[256,960]{0,1:T(8,128)(2,1)S(1)}, bf16[256,960]{0,1:T(8,128)(2,1)}, u32[]{:S(2)}) copy-start(bf16[256,960]{0,1:T(8,128)(2,1)} %copy-done.47) | copy-start | bytes 1474564
  655.8 34.5 %copy-start.137 = (f32[960]{0:T(1024)S(1)}, f32[960]{0:T(1024)}, u32[]{:S(2)}) copy-start(f32[960]{0:T(1024)} %copy-done.136) | copy-start | bytes 11524
  655.8 34.5 %copy-start.183 = (f32[256]{0:T(256)S(1)}, f32[256]{0:T(256)}, u32[]{:S(2)}) copy-start(f32[256]{0:T(256)} %get-tuple-element.2301) | copy-start | bytes 3076
  694.2 23.2 %slice-start.2 = ((s8[10485760]{0:T(1024)(128)(4,1)}), s8[2097152]{0:T(1024)(128)(4,1)S(1)}, s32[]{:S(2)}) async-start(s8[10485760]{0:T(1024)(128)(4,1)} %bitcast.870), calls=%async_computation.17 | async-start | bytes 4194304
  695.6 12.5 collective-permute-start.2
  775.1 194.5 %reduce-scatter.10.cloned.1.call-start = ((), (), s32[]{:S(2)}) async-start(), calls=%async_computation.10 | async-start | bytes 2949120 | tf_op jit(solution)/shard_map/reduce_scatter | solution.py:271
  781.7 36.0 %copy-start.103 = (bf16[256,960]{0,1:T(8,128)(2,1)}, bf16[256,960]{0,1:T(8,128)(2,1)S(1)}, u32[]{:S(2)}) copy-start(bf16[256,960]{0,1:T(8,128)(2,1)S(1)} %fusion.220) | copy-start | bytes 1474564
  781.7 32.0 %copy-start.14 = (f32[1,2,128,960]{2,1,3,0:T(2,128)S(1)}, f32[1,2,128,960]{2,1,3,0:T(2,128)}, u32[]{:S(2)}) copy-start(f32[1,2,128,960]{2,1,3,0:T(2,128)} %copy-done.12) | copy-start | bytes 2949124
  781.7 32.0 %copy-start.64 = (bf16[256,960]{0,1:T(8,128)(2,1)S(1)}, bf16[256,960]{0,1:T(8,128)(2,1)}, u32[]{:S(2)}) copy-start(bf16[256,960]{0,1:T(8,128)(2,1)} %copy-done.62) | copy-start | bytes 1474564
  781.7 32.0 %copy-start.190 = (f32[256]{0:T(256)S(1)}, f32[256]{0:T(256)}, u32[]{:S(2)}) copy-start(f32[256]{0:T(256)} %get-tuple-element.2303) | copy-start | bytes 3076
  819.4 13.0 %collective-permute-start.3 = (bf16[256,960]{0,1:T(8,128)(2,1)}, bf16[256,960]{0,1:T(8,128)(2,1)S(1)}, u32[]{:S(2)}, u32[]{:S(2)}) collective-permute-start(bf16[256,960]{0,1:T(8,128)(2,1)} %get-tuple-element.2156), channel_id=1, source_target_pairs={{16,0},{17,1},{18,2},{19,3},{20,4},{21,5},{22,6},{23,7},{24,8},{25... | collective-permute-start | bytes 1474568 | tf_op jit(solution)/shard_map/ppermute | solution.py:23
  821.6 19.2 %slice-start.5 = ((s8[10485760]{0:T(1024)(128)(4,1)}), s8[2097152]{0:T(1024)(128)(4,1)S(1)}, s32[]{:S(2)}) async-start(s8[10485760]{0:T(1024)(128)(4,1)} %bitcast.872), calls=%async_computation.20 | async-start | bytes 4194304
  899.4 199.1 %reduce-scatter.12.cloned.1.call-start = ((), (), s32[]{:S(2)}) async-start(), calls=%async_computation.11 | async-start | bytes 5849088 | tf_op jit(solution)/shard_map/reduce_scatter | solution.py:338
  1002.1 243.8 %reduce-scatter.14.cloned.1.call-start = ((), (), s32[]{:S(2)}) async-start(), calls=%async_computation.12 | async-start | bytes 16711680 | tf_op jit(solution)/shard_map/reduce_scatter | solution.py:338
  (179 other events, 721.0 us)
Sparse Core Ops, SparseCore 0:
  10.9 60.0 all-gather.13
  111.1 33.4 all-gather.7
  147.5 119.3 all-gather.15
  379.7 34.0 all-gather.9
  486.3 34.3 all-gather.11
  652.4 36.0 reduce-scatter.5
  775.2 36.7 reduce-scatter.7
  899.5 36.1 reduce-scatter.9
  1002.2 79.5 reduce-scatter.11
  1089.4 156.4 reduce-scatter.13

commit v2 on v1

v2 whole, which is shorter than its diff:
```python
import math

import jax
import jax.numpy as jnp
from jax import lax
from jax.experimental import pallas as pl
from jax.experimental.pallas import tpu as pltpu
from jax.sharding import PartitionSpec as P

D = 960
HEADS = 15
KV_HEADS = 5
HEAD_DIM = 64
SEQ_MB = 2


EPS = 1e-05
THETA = 100000.0
MASKED = -1e30


def shifted(value, axis, steps):
    count = lax.axis_size(axis)
    leading, last = (max(0, -steps), min(count, count - steps))
    return lax.ppermute(value, axis, [(source, source + steps) for source in range(leading, last)])


def rope_tables(positions):
    half_size = HEAD_DIM // 2
    exponent = jnp.arange(half_size, dtype=jnp.float32) * (2.0 / HEAD_DIM)
    frequency = jnp.exp(-exponent * math.log(THETA))
    angles = positions.astype(jnp.float32)[..., None] * frequency
    return (jnp.cos(angles), jnp.sin(angles))


def inner_rows(left, right):
    return lax.dot_general(
        left, right, (((0,), (0,)), ((), ())), preferred_element_type=jnp.float32
    )


def against(left, weight):
    return lax.dot_general(
        left, weight, (((1,), (1,)), ((), ())), preferred_element_type=jnp.float32
    )


def normalize(values, gain):
    scale = lax.rsqrt(jnp.mean(values * values, axis=-1, keepdims=True) + EPS)
    return (scale, (values * scale * gain).astype(jnp.bfloat16))


def norm_back(gradient, values, scale, gain):
    weighted = gradient * gain
    inward = scale * weighted - values * (scale * scale * scale) * jnp.mean(
        weighted * values, axis=-1, keepdims=True
    )
    return (inward, jnp.sum(gradient * values * scale, axis=0))


RATIO = HEADS // KV_HEADS
KEY_WIDTH = KV_HEADS * HEAD_DIM


def stacked_heads(ref, group):
    begin = group * RATIO
    heads = [
        ref[0, :, (begin + head) * HEAD_DIM : (begin + head + 1) * HEAD_DIM]
        for head in range(RATIO)
    ]
    return jnp.concatenate(heads, axis=0)


def allowed_pairs(mark_ref, mark_all_ref, place_ref):
    rows, length = mark_ref.shape[1], mark_all_ref.shape[2]
    key_index = lax.broadcasted_iota(jnp.int32, (rows, length), 1)
    allowed = (key_index <= place_ref[...]) & (mark_all_ref[0] == mark_ref[0])
    bias = jnp.where(allowed, 0.0, 1.0)
    return jnp.concatenate([bias] * RATIO, axis=0) > 0.5


def probabilities(queries, keys, hidden_pairs):
    scores = against(queries, keys) * HEAD_DIM ** (-0.5)
    scores = jnp.where(hidden_pairs, MASKED, scores)
    weights = jnp.exp(scores - jnp.max(scores, axis=1, keepdims=True))
    return weights * (1.0 / jnp.sum(weights, axis=1, keepdims=True))


def attend_kernel(query_ref, pack_ref, mark_ref, mark_all_ref, place_ref, mixed_ref):
    rows = query_ref.shape[1]
    hidden_pairs = allowed_pairs(mark_ref, mark_all_ref, place_ref)
    for group in range(KV_HEADS):
        begin = group * HEAD_DIM
        keys = pack_ref[0, :, begin : begin + HEAD_DIM]
        values = pack_ref[0, :, KEY_WIDTH + begin : KEY_WIDTH + begin + HEAD_DIM]
        shares = probabilities(stacked_heads(query_ref, group), keys, hidden_pairs)
        mixed = jnp.dot(
            shares.astype(jnp.bfloat16), values, preferred_element_type=jnp.float32
        ).astype(jnp.bfloat16)
        for head in range(RATIO):
            place = (group * RATIO + head) * HEAD_DIM
            mixed_ref[0, :, place : place + HEAD_DIM] = mixed[head * rows : (head + 1) * rows]


def attend_back_kernel(
    query_ref, pack_ref, mark_ref, mark_all_ref, place_ref, back_ref, back_query_ref, back_pack_ref
):
    rows = query_ref.shape[1]
    scale = HEAD_DIM ** (-0.5)
    hidden_pairs = allowed_pairs(mark_ref, mark_all_ref, place_ref)
    for group in range(KV_HEADS):
        begin = group * HEAD_DIM
        keys = pack_ref[0, :, begin : begin + HEAD_DIM]
        values = pack_ref[0, :, KEY_WIDTH + begin : KEY_WIDTH + begin + HEAD_DIM]
        queries = stacked_heads(query_ref, group)
        back = stacked_heads(back_ref, group)
        shares = probabilities(queries, keys, hidden_pairs)
        back_shares = against(back, values)
        delta = jnp.sum(shares * back_shares, axis=1, keepdims=True)
        back_scores = (shares * (back_shares - delta)).astype(jnp.bfloat16)
        back_values = inner_rows(shares.astype(jnp.bfloat16), back)
        back_keys = inner_rows(back_scores, queries) * scale
        back_queries = jnp.dot(back_scores, keys, preferred_element_type=jnp.float32) * scale
        back_pack_ref[0, :, begin : begin + HEAD_DIM] = back_keys.astype(jnp.bfloat16)
        back_pack_ref[0, :, KEY_WIDTH + begin : KEY_WIDTH + begin + HEAD_DIM] = back_values.astype(
            jnp.bfloat16
        )
        for head in range(RATIO):
            place = (group * RATIO + head) * HEAD_DIM
            back_query_ref[0, :, place : place + HEAD_DIM] = back_queries[
                head * rows : (head + 1) * rows
            ]


def sequence_spec(shape):
    return pl.BlockSpec((1,) + tuple(shape[1:]), lambda index: (index, 0, 0))


def attention_call(kernel, queries, gathered, mark, mark_all, query_index, extra, outs, products):
    count, rows, width = queries.shape
    length = gathered.shape[1]
    operands = (
        queries,
        gathered,
        mark.astype(jnp.float32)[:, :, None],
        mark_all.astype(jnp.float32)[:, None, :],
        query_index[:, None],
    ) + extra
    in_specs = [sequence_spec(operand.shape) for operand in operands]
    in_specs[4] = pl.BlockSpec((rows, 1), lambda index: (0, 0))
    pairs = count * HEADS * rows * length
    return pl.pallas_call(
        kernel,
        grid=(count,),
        in_specs=in_specs,
        out_specs=[sequence_spec(out.shape) for out in outs],
        out_shape=outs,
        compiler_params=pltpu.CompilerParams(vmem_limit_bytes=48 * 1024 * 1024),
        cost_estimate=pl.CostEstimate(
            flops=2 * products * pairs * HEAD_DIM,
            bytes_accessed=4 * (gathered.size + queries.size),
            transcendentals=pairs,
        ),
    )(*operands)


def attend(queries, gathered, mark, mark_all, query_index):
    outs = [jax.ShapeDtypeStruct(queries.shape, jnp.bfloat16)]
    return attention_call(
        attend_kernel, queries, gathered, mark, mark_all, query_index, (), outs, 2
    )[0]


def attend_back(queries, gathered, mark, mark_all, query_index, back):
    outs = [
        jax.ShapeDtypeStruct(queries.shape, jnp.float32),
        jax.ShapeDtypeStruct(gathered.shape, jnp.bfloat16),
    ]
    return attention_call(
        attend_back_kernel, queries, gathered, mark, mark_all, query_index, (back,), outs, 5
    )


def times(left, halves):
    pieces = [
        jnp.dot(left, halves[part], preferred_element_type=jnp.float32)
        for part in range(halves.shape[0])
    ]
    return jnp.concatenate(pieces, axis=1)


def times_back(left, halves):
    lanes = halves.shape[2]
    total = against(left[:, :lanes], halves[0])
    for part in range(1, halves.shape[0]):
        total = total + against(left[:, part * lanes : (part + 1) * lanes], halves[part])
    return total


def swap_halves(values):
    half = HEAD_DIM // 2
    width = values.shape[-1]
    lane = lax.broadcasted_iota(jnp.int32, values.shape, 1) % HEAD_DIM
    ahead = jnp.concatenate([values[:, half:], values[:, :half]], axis=1)
    behind = jnp.concatenate([values[:, width - half :], values[:, : width - half]], axis=1)
    return jnp.where(lane < half, ahead, behind)


def turn(values, cosine, sine):
    copies = values.shape[-1] // HEAD_DIM
    return values * jnp.tile(cosine, (1, copies)) + swap_halves(values) * jnp.tile(
        sine, (1, copies)
    )


def layer_forward(hidden, full, segment_mark, segment_all, cosine, sine, query_index):
    qkv_weight, out_weight, gate_weight, up_weight, down_weight, gains = full
    count, local_length = segment_mark.shape
    rows = hidden.shape[0]
    key_width = KV_HEADS * HEAD_DIM
    query_width = HEADS * HEAD_DIM
    scale_front, normed = normalize(hidden, gains[0])
    qkv = times_back(normed, qkv_weight)
    turned = turn(qkv[:, : query_width + key_width], cosine, sine).astype(jnp.bfloat16)
    values = qkv[:, query_width + key_width :].astype(jnp.bfloat16)
    packed = jnp.concatenate([turned[:, query_width:], values], axis=-1)
    gathered = lax.all_gather(
        packed.reshape(count, local_length, 2 * key_width), "seq", axis=1, tiled=True
    )
    query_view = turned[:, :query_width].reshape(count, local_length, query_width)
    mixed_low = attend(query_view, gathered, segment_mark, segment_all, query_index)
    mixed_low = mixed_low.reshape(rows, query_width)
    middle = hidden + times(mixed_low, out_weight)
    scale_back, normed_back = normalize(middle, gains[1])
    gate = times_back(normed_back, gate_weight)
    upward = times_back(normed_back, up_weight)
    product = (gate * jax.nn.sigmoid(gate) * upward).astype(jnp.bfloat16)
    output = middle + times(product, down_weight)
    kept = (
        hidden,
        scale_front,
        normed,
        query_view,
        gathered,
        mixed_low,
        middle,
        scale_back,
        normed_back,
        gate,
        upward,
        product,
    )
    return (output, kept)


def layer_backward(incoming_low, full, kept, segment_mark, segment_all, cosine, sine, query_index):
    qkv_weight, out_weight, gate_weight, up_weight, down_weight, gains = full
    (
        hidden,
        scale_front,
        normed,
        query_view,
        gathered,
        mixed_low,
        middle,
        scale_back,
        normed_back,
        gate,
        upward,
        product,
    ) = kept
    rows = hidden.shape[0]
    key_width = KV_HEADS * HEAD_DIM
    query_width = HEADS * HEAD_DIM
    incoming = incoming_low.astype(jnp.float32)
    back_product = times_back(incoming_low, down_weight)
    sigma = jax.nn.sigmoid(gate)
    back_gate = (back_product * upward * sigma * (1.0 + gate * (1.0 - sigma))).astype(jnp.bfloat16)
    back_up = (back_product * gate * sigma).astype(jnp.bfloat16)
    back_normed = times(back_gate, gate_weight) + times(back_up, up_weight)
    inward, gain_back_grad = norm_back(back_normed, middle, scale_back, gains[1])
    back_middle = incoming + inward
    branch = back_middle.astype(jnp.bfloat16)
    back_mixed = times_back(branch, out_weight).astype(jnp.bfloat16)
    back_view = back_mixed.reshape(query_view.shape)
    back_query, buffer = attend_back(
        query_view, gathered, segment_mark, segment_all, query_index, back_view
    )
    summed = lax.psum_scatter(
        buffer, "seq", scatter_dimension=1, tiled=True
    ).reshape(rows, 2 * key_width)
    back_queries = turn(back_query.reshape(rows, query_width), cosine, -sine).astype(jnp.bfloat16)
    back_keys = turn(summed[:, :key_width].astype(jnp.float32), cosine, -sine).astype(jnp.bfloat16)
    back_qkv = jnp.concatenate([back_queries, back_keys, summed[:, key_width:]], axis=1)
    back_front = times(back_qkv, qkv_weight)
    inward_front, gain_front_grad = norm_back(back_front, hidden, scale_front, gains[0])
    back_hidden = back_middle + inward_front
    gains_grad = jnp.stack([gain_front_grad, gain_back_grad])
    terms = (
        normed,
        back_qkv,
        mixed_low,
        branch,
        normed_back,
        back_gate,
        back_up,
        product,
        incoming_low,
    )
    return (back_hidden, terms, gains_grad)


GAIN_ROWS = 16


def gather_weights(shards):
    query_part, key_part, value_part, out_part, gate_part, up_part, down_part, gain_part = shards
    seq = lax.axis_size("seq")
    dp = lax.axis_size("dp")
    lanes = query_part.shape[0]
    heights = (query_part.shape[1], key_part.shape[1], value_part.shape[1], out_part.shape[0])
    gain_block = jnp.pad(
        gain_part, ((0, GAIN_ROWS - gain_part.shape[0]), (0, lanes - gain_part.shape[1]))
    )
    front = jnp.concatenate(
        [
            jnp.concatenate([query_part, key_part, value_part], axis=1).T,
            out_part,
            gain_block,
        ],
        axis=0,
    )
    step = gate_part.shape[1]
    rear = jnp.concatenate([gate_part, up_part], axis=1).T.reshape(2, step, lanes)
    rear = jnp.concatenate([rear, down_part[None]], axis=0)
    front_all = lax.all_gather(front, ("seq", "dp"), axis=0, tiled=False)
    front_all = front_all.reshape(seq, dp, front.shape[0], lanes)
    rear_all = lax.all_gather(rear, ("dp", "seq"), axis=1, tiled=True)
    rear_all = rear_all.reshape(3, dp, seq * step, lanes)

    def whole(block, begin, size):
        piece = lax.slice_in_dim(block, begin, begin + size, axis=2)
        return piece.transpose(1, 0, 2, 3).reshape(dp, seq * size, lanes)

    places = [0]
    for height in heights:
        places.append(places[-1] + height)
    qkv = jnp.concatenate([whole(front_all, places[i], heights[i]) for i in range(3)], axis=1)
    out = whole(front_all, places[3], heights[3])
    gain_width = gain_part.shape[1]
    gains = lax.slice(
        front_all, (0, 0, places[4], 0), (seq, 1, places[4] + gain_part.shape[0], gain_width)
    )
    gains = gains[:, 0].transpose(1, 0, 2).reshape(gain_part.shape[0], seq * gain_width)
    return (qkv, out, rear_all[0], rear_all[1], rear_all[2], gains.astype(jnp.float32))


def outer(left, right, dp):
    lanes = right.shape[1] // dp
    return [
        inner_rows(left, right[:, part * lanes : (part + 1) * lanes]).astype(jnp.bfloat16)
        for part in range(dp)
    ]


def reduce_grads(terms, gains_grad):
    normed, back_qkv, mixed_low, branch, normed_back, back_gate, back_up, product, incoming = terms
    seq = lax.axis_size("seq")
    dp = lax.axis_size("dp")
    key_width = KV_HEADS * HEAD_DIM
    query_width = HEADS * HEAD_DIM
    pairs = ((back_gate, normed_back), (back_up, normed_back), (product, incoming))
    pieces = [piece for left, right in pairs for piece in outer(left, right, dp)]
    hidden_width, lanes = pieces[0].shape
    rear = jnp.concatenate(pieces, axis=0).reshape(len(pairs), dp * hidden_width, lanes)
    rear = lax.psum_scatter(rear, ("dp", "seq"), scatter_dimension=1, tiled=True)
    rear = rear.astype(jnp.float32)
    qkv = jnp.stack(outer(back_qkv, normed, dp))
    out = jnp.stack(outer(mixed_low, branch, dp))
    gain_kinds, gain_all = gains_grad.shape
    gain_width = gain_all // seq
    gain_block = gains_grad.astype(jnp.bfloat16).reshape(gain_kinds, seq, gain_width)
    gain_block = gain_block.transpose(1, 0, 2)
    gain_block = jnp.pad(
        gain_block, ((0, 0), (0, GAIN_ROWS - gain_kinds), (0, lanes - gain_width))
    )
    gain_block = jnp.broadcast_to(gain_block[None], (dp, seq, GAIN_ROWS, lanes))

    def split_rows(block):
        return block.reshape(dp, seq, block.shape[1] // seq, lanes)

    front = jnp.concatenate(
        [
            split_rows(qkv[:, :query_width]),
            split_rows(qkv[:, query_width : query_width + key_width]),
            split_rows(qkv[:, query_width + key_width :]),
            split_rows(out),
            gain_block,
        ],
        axis=2,
    )
    height = front.shape[2]
    front = lax.psum_scatter(
        front.reshape(dp * seq * height, lanes), ("dp", "seq"), scatter_dimension=0, tiled=True
    ).astype(jnp.float32)
    query_rows = query_width // seq
    key_rows = key_width // seq
    first = query_rows + key_rows
    second = first + key_rows
    third = second + query_rows
    return (
        front[:query_rows].T,
        front[query_rows:first].T,
        front[first:second].T,
        front[second:third],
        rear[0].T,
        rear[1].T,
        rear[2],
        front[third : third + gain_kinds, :gain_width],
    )


def pick_section(section, early, late):

    def select(early_part, late_part):
        return jnp.where(section == 0, early_part, late_part)

    return jax.tree.map(select, early, late)


def on_device(
    ends,
    segments,
    positions,
    query_weights,
    key_weights,
    value_weights,
    out_weights,
    gate_weights,
    up_weights,
    down_weights,
    norm_gains,
):
    section = lax.axis_index("section")
    sections = lax.axis_size("section")
    count = SEQ_MB
    micro = segments.shape[0] // count
    local_length = segments.shape[1]
    rows = count * local_length
    ticks = micro + sections - 1
    query_index = lax.axis_index("seq") * local_length + jnp.arange(local_length)
    shards = (
        query_weights[0],
        key_weights[0],
        value_weights[0],
        out_weights[0],
        gate_weights[0],
        up_weights[0],
        down_weights[0],
        norm_gains[0],
    )
    full = gather_weights(shards)
    outside = ends[0].reshape(micro, rows, D)
    blank = jnp.zeros((rows, D), jnp.bfloat16)

    marks = segments.astype(jnp.bfloat16)
    marks_all = lax.all_gather(marks, "seq", axis=1, tiled=True)
    cosines, sines = rope_tables(positions.reshape(micro * rows))
    cosines = jnp.concatenate([cosines, cosines], axis=1)
    sines = jnp.concatenate([-sines, sines], axis=1)

    def batch_inputs(index):
        mark = lax.dynamic_slice_in_dim(marks, index * count, count, 0)
        mark_all = lax.dynamic_slice_in_dim(marks_all, index * count, count, 0)
        cosine = lax.dynamic_slice_in_dim(cosines, index * rows, rows, 0)
        sine = lax.dynamic_slice_in_dim(sines, index * rows, rows, 0)
        return (mark, mark_all, cosine, sine)

    received = blank
    results = []
    stores = []
    for tick in range(ticks):
        own = outside[tick] if tick < micro else blank
        source = jnp.where(section == 0, own, received)
        index = jnp.clip(tick - section, 0, micro - 1)
        mark, mark_all, cosine, sine = batch_inputs(index)
        output, kept = layer_forward(
            source.astype(jnp.float32), full, mark, mark_all, cosine, sine, query_index
        )
        sent = output.astype(jnp.bfloat16)
        results.append(sent)
        stores.append(kept)
        if tick + 1 < ticks:
            received = shifted(sent, "section", 1)
    received = blank
    sent_back = []
    collected = []
    gains_grad = 0.0
    for tick in range(ticks):
        own = outside[tick] if tick < micro else blank
        incoming = jnp.where(section == sections - 1, own, received)
        index = jnp.clip(tick - 1 + section, 0, micro - 1)
        mark, mark_all, cosine, sine = batch_inputs(index)
        kept = pick_section(section, stores[max(tick - 1, 0)], stores[min(tick + 1, ticks - 1)])
        back_hidden, terms, gains_part = layer_backward(
            incoming, full, kept, mark, mark_all, cosine, sine, query_index
        )
        collected.append(terms)
        gains_grad = gains_grad + gains_part
        sent = back_hidden.astype(jnp.bfloat16)
        sent_back.append(sent)
        if tick + 1 < ticks:
            received = shifted(sent, "section", -1)
    terms = tuple(jnp.concatenate(parts, axis=0) for parts in zip(*collected))
    totals = reduce_grads(terms, gains_grad)
    outputs_list = []
    grads_list = []
    for batch in range(micro):
        outputs_list.append(
            jnp.where(section == 0, results[batch], results[batch + 1]).reshape(
                count, local_length, D
            )
        )
        grads_list.append(
            jnp.where(section == 0, sent_back[batch + 1], sent_back[batch]).reshape(
                count, local_length, D
            )
        )
    activations = jnp.concatenate(outputs_list, axis=0)[None]
    input_grads = jnp.concatenate(grads_list, axis=0)[None]
    return (
        activations,
        input_grads,
        totals[0][None],
        totals[1][None],
        totals[2][None],
        totals[3][None],
        totals[4][None],
        totals[5][None],
        totals[6][None],
        totals[7][None],
    )


def solution(mesh):
    return jax.shard_map(
        on_device,
        mesh=mesh,
        in_specs=(
            P("section", "dp", "seq", None),
            P("dp", "seq"),
            P("dp", "seq"),
            P("section", "dp", "seq"),
            P("section", "dp", "seq"),
            P("section", "dp", "seq"),
            P("section", "seq", "dp"),
            P("section", "dp", "seq"),
            P("section", "dp", "seq"),
            P("section", "seq", "dp"),
            P("section", None, "seq"),
        ),
        out_specs=(
            P("section", "dp", "seq", None),
            P("section", "dp", "seq", None),
            P("section", "dp", "seq"),
            P("section", "dp", "seq"),
            P("section", "dp", "seq"),
            P("section", "seq", "dp"),
            P("section", "dp", "seq"),
            P("section", "dp", "seq"),
            P("section", "seq", "dp"),
            P("section", None, "seq"),
        ),
        check_vma=False,
    )
```

time: 1270 us -> 980 us (0.77)
  local copies, waits for them, and re-layouts: 332 us -> 124 us
  matrix products: 297 us -> 140 us
  Pallas kernels: 0 us -> 97.4 us
  other arithmetic: 127 us -> 71.6 us
  waiting for transfers between devices: 458 us -> 502 us
    dot_general x54 -> x30, matrix products: 207 us -> 41.9 us  [times(): jnp.dot(left, halves[part], preferred_element_type=jnp.float32)]
    reshape x26 -> x7, local copies, waits for them, and re-layouts: 134 us -> 8.37 us  [the longest x3 2.95 us: layer_forward(): mixed_low = mixed_low.reshape(rows, query_width)]
    pallas_call x0 -> x6, Pallas kernels: none -> 97.4 us  [attention_call(): pl.pallas_call(kernel, grid=(count,), in_specs=in_specs, out_specs=[seque...]
    reduce_scatter x5, waiting for transfers between devices: 207 us -> 249 us  [the longest x1 157 us: reduce_grads(): lax.psum_scatter(rear, ('dp', 'seq'), scatter_dimension=1, tiled=True)]
    transpose x7 -> x5, local copies, waits for them, and re-layouts: 43.4 us -> 5.97 us  [whole(): return piece.transpose(1, 0, 2, 3).reshape(dp, seq * size, lanes)]
    slice x28 -> x11, local copies, waits for them, and re-layouts: 46.3 us -> 10.1 us  [the longest x1 2.93 us: times(): halves[part]]
    reduce_sum x6, other arithmetic: 29.6 us -> 2.81 us  [norm_back(): return (inward, jnp.sum(gradient * values * scale, axis=0))]
    all_gather x1, waiting for transfers between devices: 83.4 us -> 102 us  [gather_weights(): rear_all = lax.all_gather(rear, ('dp', 'seq'), axis=1, tiled=True)]
  transfers between devices with their start and end apart: 14 -> 14, of which waited for: 12 -> 14; matrix products, arithmetic and copies ran while one was open for 19% -> 14% of each run, Pallas kernels for 0% -> 1%
where the time goes in v2:
time: 980 us; the launch traced here: 975 us
  waiting for transfers between devices  502 us (51%)
  matrix products  140 us (14%)
  local copies, waits for them, and re-layouts  124 us (13%)
  Pallas kernels  97.4 us (10%)
  other arithmetic  71.6 us (7%)
  between operations  17.9 us (2%)
  starting transfers between devices  11.3 us (1%)
  blocking collectives  10.5 us (1%)
    reduce_scatter x1, waiting for transfers between devices, reduce_grads(): lax.psum_scatter(rear, ('dp', 'seq'), scatter_dimension=1, tiled=True)  157 us
    all_gather x1, waiting for transfers between devices, gather_weights(): rear_all = lax.all_gather(rear, ('dp', 'seq'), axis=1, tiled=True)  102 us
    pallas_call x6, Pallas kernels, attention_call(): pl.pallas_call(kernel, grid=(count,), in_specs=in_specs, out_specs=[seque...  97.4 us
    dot_general x30, matrix products, against(): lax.dot_general(left, weight, (((1,), (1,)), ((), ())), preferred_element...  70.8 us
    reduce_scatter x3, waiting for transfers between devices, layer_backward(): lax.psum_scatter(buffer, 'seq', scatter_dimension=1, tiled=True)  68.8 us
    all_gather x3, waiting for transfers between devices, layer_forward(): lax.all_gather(packed.reshape(count, local_length, 2 * key_width), 'seq',...  60 us
    all_gather x1, waiting for transfers between devices, gather_weights(): front_all = lax.all_gather(front, ('seq', 'dp'), axis=0, tiled=False)  55.1 us
    unnamed x478, local copies, waits for them, and re-layouts  47.7 us
  transfers between devices with their start and end apart: 14, of which 14 were waited for; matrix products, arithmetic and copies ran while one was open for 14% of the time, Pallas kernels for 1%

profile of v2, /device:TPU:0, one launch (start us, length us, event | category | flops | bytes accessed | tf_op | source)
XLA Modules:
  0.0 974.6 jit_solution(13299295505896996712)
XLA Ops:
  15.9 55.1 %all-gather.15.cloned.1.call-done = bf16[5376,480]{1,0:T(8,128)(2,1)} async-done(((bf16[336,480]{1,0:T(8,128)(2,1)}), bf16[5376,480]{1,0:T(8,128)(2,1)}) %all-gather.15.cloned.1.call-update) | async-done | bytes 5160976 | tf_op jit(solution)/shard_map/all_gather | solution.py:336
  73.1 4.4 slice_bitcast_fusion.6
  84.8 10.5 %all_gather.24 = bf16[4,1024]{1,0:T(4,128)(2,1)S(1)} all-gather(bf16[4,128]{1,0:T(4,128)(2,1)S(1)} %convert_element_type.234), channel_id=1, replica_groups=mesh['section'=2,'dp'=2,'seq'=8] {'seq'}, dimensions={1}, use_global_device_ids=true | all-gather | bytes 9216 | tf_op jit(solution)/shard_map/all_gather | solution.py:467
  96.4 2.9 fusion.213
  99.3 16.7 %all-gather.7.cloned.1.call-done.pack_ref = bf16[2,1024,640]{2,1,0:T(8,128)(2,1)} async-done(((bf16[2,128,640]{2,1,0:T(8,128)(2,1)}), bf16[2,1024,640]{2,1,0:T(8,128)(2,1)}) %all-gather.7.cloned.1.call-update) | async-done | bytes 2621456 | tf_op jit(solution)/shard_map/all_gather | solution.py:227
  117.8 9.9 %shard_map.186 = bf16[2,128,960]{2,1,0:T(8,128)(2,1)S(1)} custom-call(bf16[2,128,960]{2,1,0:T(8,128)(2,1)S(1)} %bitcast.415, bf16[2,1024,640]{2,1,0:T(8,128)(2,1)S(1)} %copy-done.5, f32[2,128,1]{2,1,0:T(8,128)S(1)} %copy.156.mark_ref, f32[2,1,1024]{2,1,0:T(1,128)S(1)} %copy.157.mark_all_ref, s32[128,1]{1,0:T(8,128)S(1)} %iota_add_fusion.place_ref), custom_call_target="tpu_custom_call" | custom-call | flops 1006632960 | bytes 6225920 | tf_op jit(solution)/shard_map/pallas_call | solution.py:152
  135.6 102.0 %all-gather.9.cloned.1.call-done = bf16[3,5120,480]{2,1,0:T(8,128)(2,1)} async-done(((bf16[3,320,480]{2,1,0:T(8,128)(2,1)}), bf16[3,5120,480]{2,1,0:T(8,128)(2,1)}) %all-gather.9.cloned.1.call-update) | async-done | bytes 14745616 | tf_op jit(solution)/shard_map/all_gather | solution.py:338
  240.4 3.2 fusion.26
  251.5 3.7 collective-permute-start
  255.7 10.3 %collective-permute-done = bf16[256,960]{0,1:T(8,128)(2,1)S(1)} collective-permute-done((bf16[256,960]{0,1:T(8,128)(2,1)S(1)}, bf16[256,960]{0,1:T(8,128)(2,1)S(1)}, u32[]{:S(2)}, u32[]{:S(2)}) %collective-permute-start) | collective-permute-done | bytes 491552 | tf_op jit(solution)/shard_map/ppermute | solution.py:25
  272.6 31.7 %all-gather.11.cloned.1.call-done.pack_ref = bf16[2,1024,640]{2,1,0:T(8,128)(2,1)} async-done(((bf16[2,128,640]{2,1,0:T(8,128)(2,1)}), bf16[2,1024,640]{2,1,0:T(8,128)(2,1)}) %all-gather.11.cloned.1.call-update) | async-done | bytes 2621456 | tf_op jit(solution)/shard_map/all_gather | solution.py:227
  306.0 19.9 %shard_map.187 = bf16[2,128,960]{2,1,0:T(8,128)(2,1)S(1)} custom-call(bf16[2,128,960]{2,1,0:T(8,128)(2,1)S(1)} %bitcast.417, bf16[2,1024,640]{2,1,0:T(8,128)(2,1)S(1)} %copy-done.6, f32[2,128,1]{2,1,0:T(8,128)S(1)} %copy.163.mark_ref, f32[2,1,1024]{2,1,0:T(1,128)S(1)} %copy.164.mark_all_ref, s32[128,1]{1,0:T(8,128)S(1)} %iota_add_fusion.place_ref), custom_call_target="tpu_custom_call" | custom-call | flops 1006632960 | bytes 6225920 | tf_op jit(solution)/shard_map/pallas_call | solution.py:152
  328.4 2.9 fusion.34
  331.3 2.8 fusion.25
  336.9 3.3 broadcast_select_fusion.5
  343.7 3.5 collective-permute-start.1
  347.2 10.8 %collective-permute-done.1 = bf16[256,960]{0,1:T(8,128)(2,1)S(1)} collective-permute-done((bf16[256,960]{0,1:T(8,128)(2,1)S(1)}, bf16[256,960]{0,1:T(8,128)(2,1)S(1)}, u32[]{:S(2)}, u32[]{:S(2)}) %collective-permute-start.1) | collective-permute-done | bytes 491552 | tf_op jit(solution)/shard_map/ppermute | solution.py:25
  366.8 3.0 fusion.39
  370.3 5.2 multiply_convert_fusion.5
  387.0 11.6 %all-gather.13.cloned.1.call-done.pack_ref = bf16[2,1024,640]{2,1,0:T(8,128)(2,1)} async-done(((bf16[2,128,640]{2,1,0:T(8,128)(2,1)}), bf16[2,1024,640]{2,1,0:T(8,128)(2,1)}) %all-gather.13.cloned.1.call-update) | async-done | bytes 2621456 | tf_op jit(solution)/shard_map/all_gather | solution.py:227
  400.3 10.0 %shard_map.188 = bf16[2,128,960]{2,1,0:T(8,128)(2,1)S(1)} custom-call(bf16[2,128,960]{2,1,0:T(8,128)(2,1)S(1)} %bitcast.420, bf16[2,1024,640]{2,1,0:T(8,128)(2,1)S(1)} %copy-done.7, f32[2,128,1]{2,1,0:T(8,128)S(1)} %copy.167.mark_ref, f32[2,1,1024]{2,1,0:T(1,128)S(1)} %copy.168.mark_all_ref, s32[128,1]{1,0:T(8,128)S(1)} %iota_add_fusion.place_ref), custom_call_target="tpu_custom_call" | custom-call | flops 1006632960 | bytes 6225920 | tf_op jit(solution)/shard_map/pallas_call | solution.py:152
  417.6 5.5 broadcast_select_fusion
  423.2 19.0 %shard_map.189 = (f32[2,128,960]{2,1,0:T(8,128)S(1)}, bf16[2,1024,640]{2,1,0:T(8,128)(2,1)S(1)}) custom-call(bf16[2,128,960]{2,1,0:T(8,128)(2,1)S(1)} %copy-done.9, bf16[2,1024,640]{2,1,0:T(8,128)(2,1)} %get-tuple-element.100.pack_ref, f32[2,128,1]{2,1,0:T(8,128)S(1)} %copy.173.mark_ref, f32[2,1,1024]{2,1,0:T(1,128)S(1)} %copy.174.mark_all_ref, ...), custom_call_target="tpu_custom_call" | custom-call | flops 2516582400 | bytes 6225920 | tf_op jit(solution)/shard_map/pallas_call | solution.py:152
  450.7 4.3 fusion.33
  457.7 4.2 convolution_add_fusion.4
  461.9 18.5 %reduce-scatter.6.cloned.1.call-done = bf16[2,128,640]{2,1,0:T(8,128)(2,1)} async-done(((bf16[2,1024,640]{2,1,0:T(8,128)(2,1)}), bf16[2,128,640]{2,1,0:T(8,128)(2,1)}) %reduce-scatter.6.cloned.1.call-update) | async-done | bytes 327696 | tf_op jit(solution)/shard_map/reduce_scatter | solution.py:289
  490.0 7.9 broadcast_select_fusion.4
  497.8 3.0 collective-permute-done.2
  503.7 3.5 multiply_convert_fusion.3
  518.9 19.3 %shard_map.190 = (f32[2,128,960]{2,1,0:T(8,128)S(1)}, bf16[2,1024,640]{2,1,0:T(8,128)(2,1)S(1)}) custom-call(bf16[2,128,960]{2,1,0:T(8,128)(2,1)S(1)} %copy-done.8, bf16[2,1024,640]{2,1,0:T(8,128)(2,1)} %get-tuple-element.99.pack_ref, f32[2,128,1]{2,1,0:T(8,128)S(1)} %copy.183.mark_ref, f32[2,1,1024]{2,1,0:T(1,128)S(1)} %copy.184.mark_all_ref, ...), custom_call_target="tpu_custom_call" | custom-call | flops 2516582400 | bytes 6225920 | tf_op jit(solution)/shard_map/pallas_call | solution.py:152
  544.3 32.2 %reduce-scatter.8.cloned.1.call-done = bf16[2,128,640]{2,1,0:T(8,128)(2,1)} async-done(((bf16[2,1024,640]{2,1,0:T(8,128)(2,1)}), bf16[2,128,640]{2,1,0:T(8,128)(2,1)}) %reduce-scatter.8.cloned.1.call-update) | async-done | bytes 327696 | tf_op jit(solution)/shard_map/reduce_scatter | solution.py:289
  587.2 11.1 %collective-permute-done.3 = bf16[256,960]{0,1:T(8,128)(2,1)S(1)} collective-permute-done((bf16[256,960]{0,1:T(8,128)(2,1)}, bf16[256,960]{0,1:T(8,128)(2,1)S(1)}, u32[]{:S(2)}, u32[]{:S(2)}) %collective-permute-start.3) | collective-permute-done | bytes 491552 | tf_op jit(solution)/shard_map/ppermute | solution.py:25
  598.4 3.0 fusion.43
  602.0 4.7 multiply_convert_fusion.1
  619.5 19.3 %shard_map.191 = (f32[2,128,960]{2,1,0:T(8,128)S(1)}, bf16[2,1024,640]{2,1,0:T(8,128)(2,1)S(1)}) custom-call(bf16[2,128,960]{2,1,0:T(8,128)(2,1)S(1)} %get-tuple-element.136.query_ref, bf16[2,1024,640]{2,1,0:T(8,128)(2,1)} %get-tuple-element.98.pack_ref, f32[2,128,1]{2,1,0:T(8,128)S(1)} %copy.193.mark_ref, f32[2,1,1024]{2,1,0:T(1,128)S(1)} %reshape.502.mark_all_ref, ...), custom_call_target="tpu_custom_call" | custom-call | flops 2516582400 | bytes 6225920 | tf_op jit(solution)/shard_map/pallas_call | solution.py:152
  659.0 18.1 %reduce-scatter.10.cloned.1.call-done = bf16[2,128,640]{2,1,0:T(8,128)(2,1)} async-done(((bf16[2,1024,640]{2,1,0:T(8,128)(2,1)}), bf16[2,128,640]{2,1,0:T(8,128)(2,1)}) %reduce-scatter.10.cloned.1.call-update) | async-done | bytes 327696 | tf_op jit(solution)/shard_map/reduce_scatter | solution.py:289
  688.0 17.2 %maximum_maximum_fusion = bf16[768,1600]{0,1:T(8,128)(2,1)S(1)} fusion(bf16[256,320]{0,1:T(8,128)(2,1)S(1)} %copy-done.147, bf16[256,320]{0,1:T(8,128)(2,1)S(1)} %fusion.104, bf16[256,960]{0,1:T(8,128)(2,1)S(1)} %copy-done.131, bf16[256,320]{0,1:T(8,128)(2,1)S(1)} %copy-done.146, bf16[256,320]{0,1:T(8,128)(2,1)S(1)} %copy-done.151, ...), kind=kLoop, calls=%fused_computation.57 | loop fusion | flops 22118400 | bytes 4915200 | tf_op jit(solution)/shard_map/concatenate | solution.py:514
  728.6 3.5 fusion.5
  732.1 3.4 fusion.4
  735.5 3.4 fusion.3
  738.9 3.4 fusion.2
  742.3 3.4 fusion.1
  745.7 3.3 fusion
  749.0 19.1 %copy.214 = bf16[15360,480]{1,0:T(8,128)(2,1)} copy(bf16[15360,480]{0,1:T(8,128)(2,1)} %fusion) | data formatting | bytes 29491200 | tf_op jit(solution)/shard_map/concatenate | solution.py:375
  769.6 2.9 fusion.45
  772.5 3.0 fusion.40
  779.7 23.8 %reduce-scatter.12.cloned.1.call-done = bf16[336,480]{1,0:T(8,128)(2,1)} async-done(((bf16[5376,480]{1,0:T(8,128)(2,1)}), bf16[336,480]{1,0:T(8,128)(2,1)}) %reduce-scatter.12.cloned.1.call-update) | async-done | bytes 322576 | tf_op jit(solution)/shard_map/reduce_scatter | solution.py:403
  807.3 156.5 %reduce-scatter.14.cloned.1.call-done = bf16[3,320,480]{2,1,0:T(8,128)(2,1)} async-done(((bf16[3,5120,480]{2,1,0:T(8,128)(2,1)}), bf16[3,320,480]{2,1,0:T(8,128)(2,1)}) %reduce-scatter.14.cloned.1.call-update) | async-done | bytes 921616 | tf_op jit(solution)/shard_map/reduce_scatter | solution.py:376
  (737 shorter events, 216.9 us)
Async XLA Ops:
  7.2 63.8 %all-gather.15.cloned.1.call-start = ((), (), s32[]{:S(2)}) async-start(), calls=%async_computation.14 | async-start | bytes 5849088 | tf_op jit(solution)/shard_map/all_gather | solution.py:336
  10.8 105.2 %all-gather.7.cloned.1.call-start = ((), (), s32[]{:S(2)}) async-start(), calls=%async_computation.5 | async-start | bytes 2949120 | tf_op jit(solution)/shard_map/all_gather | solution.py:227
  14.0 344.9 %copy-start.10 = (f32[1,2,128,960]{2,1,3,0:T(2,128)}, f32[1,2,128,960]{2,1,3,0:T(2,128)S(1)}, u32[]{:S(2)}) copy-start(f32[1,2,128,960]{2,1,3,0:T(2,128)S(1)} %copy.149) | copy-start | bytes 2949124
  83.4 154.2 %all-gather.9.cloned.1.call-start = ((), (), s32[]{:S(2)}) async-start(), calls=%async_computation.6 | async-start | bytes 16711680 | tf_op jit(solution)/shard_map/all_gather | solution.py:338
  84.7 219.6 %all-gather.11.cloned.1.call-start = ((), (), s32[]{:S(2)}) async-start(), calls=%async_computation.7 | async-start | bytes 2949120 | tf_op jit(solution)/shard_map/all_gather | solution.py:227
  117.8 9.9 %copy-start.29 = (bf16[1,8,120,480]{3,2,0,1:T(8,128)(2,1)S(1)}, bf16[1,8,120,480]{3,2,0,1:T(8,128)(2,1)}, u32[]{:S(2)}) copy-start(bf16[1,8,120,480]{3,2,0,1:T(8,128)(2,1)} %get-tuple-element.103) | copy-start | bytes 2764804
  135.6 110.8 %copy-start.53 = (bf16[256,960]{0,1:T(8,128)(2,1)}, bf16[256,960]{0,1:T(8,128)(2,1)S(1)}, u32[]{:S(2)}) copy-start(bf16[256,960]{0,1:T(8,128)(2,1)S(1)} %get-tuple-element.84) | copy-start | bytes 1474564
  251.5 14.6 %copy-start.116 = (bf16[256,960]{0,1:T(8,128)(2,1)}, bf16[256,960]{0,1:T(8,128)(2,1)S(1)}, u32[]{:S(2)}) copy-start(bf16[256,960]{0,1:T(8,128)(2,1)S(1)} %fusion.58) | copy-start | bytes 1474564
  251.5 15.9 %copy-start.20 = (bf16[2,1600,480]{2,1,0:T(8,128)(2,1)S(1)}, bf16[2,1600,480]{2,1,0:T(8,128)(2,1)}, u32[]{:S(2)}) copy-start(bf16[2,1600,480]{2,1,0:T(8,128)(2,1)} %copy-done.19) | copy-start | bytes 9216004
  251.5 14.5 %collective-permute-start = (bf16[256,960]{0,1:T(8,128)(2,1)S(1)}, bf16[256,960]{0,1:T(8,128)(2,1)S(1)}, u32[]{:S(2)}, u32[]{:S(2)}) collective-permute-start(bf16[256,960]{0,1:T(8,128)(2,1)S(1)} %fusion.58), channel_id=1, source_target_pairs={{0,16},{1,17},{2,18},{3,19},{4,20},{5,21},{6,22},{7,23},{8,24},{9,... | collective-permute-start | bytes 1474568 | tf_op jit(solution)/shard_map/ppermute | solution.py:25
  255.7 10.6 %copy-start.91 = (bf16[1,2,128,960]{2,1,3,0:T(2,128)(2,1)}, bf16[1,2,128,960]{2,1,3,0:T(2,128)(2,1)S(1)}, u32[]{:S(2)}) copy-start(bf16[1,2,128,960]{2,1,3,0:T(2,128)(2,1)S(1)} %copy.160) | copy-start | bytes 1474564
  266.3 76.3 %copy-start.14 = (bf16[256,960]{0,1:T(8,128)(2,1)}, bf16[256,960]{0,1:T(8,128)(2,1)S(1)}, u32[]{:S(2)}) copy-start(bf16[256,960]{0,1:T(8,128)(2,1)S(1)} %get-tuple-element.83) | copy-start | bytes 1474564
  271.1 127.5 %all-gather.13.cloned.1.call-start = ((), (), s32[]{:S(2)}) async-start(), calls=%async_computation.8 | async-start | bytes 2949120 | tf_op jit(solution)/shard_map/all_gather | solution.py:227
  306.0 19.9 %copy-start.25 = (bf16[1,8,120,480]{3,2,0,1:T(8,128)(2,1)S(1)}, bf16[1,8,120,480]{3,2,0,1:T(8,128)(2,1)}, u32[]{:S(2)}) copy-start(bf16[1,8,120,480]{3,2,0,1:T(8,128)(2,1)} %get-tuple-element.104) | copy-start | bytes 2764804
  306.0 20.5 %copy-start.30 = (bf16[1,8,120,480]{3,2,0,1:T(8,128)(2,1)S(1)}, bf16[1,8,120,480]{3,2,0,1:T(8,128)(2,1)}, u32[]{:S(2)}) copy-start(bf16[1,8,120,480]{3,2,0,1:T(8,128)(2,1)} %get-tuple-element.103) | copy-start | bytes 2764804
  306.0 30.8 %slice-start = ((s8[15728640]{0:T(1024)(128)(4,1)}), s8[3145728]{0:T(1024)(128)(4,1)S(1)}, s32[]{:S(2)}) async-start(s8[15728640]{0:T(1024)(128)(4,1)} %bitcast.435), calls=%async_computation.15 | async-start | bytes 6291456
  326.0 10.9 %slice-start.1 = ((s8[15728640]{0:T(1024)(128)(4,1)}), s8[4194304]{0:T(1024)(128)(4,1)S(1)}, s32[]{:S(2)}) async-start(s8[15728640]{0:T(1024)(128)(4,1)} %bitcast.435), calls=%async_computation.16 | async-start | bytes 8388608
  326.5 16.0 %copy-start.42 = (f32[256,480]{0,1:T(8,128)}, f32[256,480]{0,1:T(8,128)S(1)}, u32[]{:S(2)}) copy-start(f32[256,480]{0,1:T(8,128)S(1)} %fusion.238) | copy-start | bytes 1474564
  327.1 15.5 %copy-start.45 = (f32[256,480]{0,1:T(8,128)}, f32[256,480]{0,1:T(8,128)S(1)}, u32[]{:S(2)}) copy-start(f32[256,480]{0,1:T(8,128)S(1)} %fusion.237) | copy-start | bytes 1474564
  342.6 17.3 %copy-start.21 = (bf16[2,1600,480]{2,1,0:T(8,128)(2,1)S(1)}, bf16[2,1600,480]{2,1,0:T(8,128)(2,1)}, u32[]{:S(2)}) copy-start(bf16[2,1600,480]{2,1,0:T(8,128)(2,1)} %copy-done.19) | copy-start | bytes 9216004
  343.7 16.8 %copy-start.113 = (bf16[256,960]{0,1:T(8,128)(2,1)}, bf16[256,960]{0,1:T(8,128)(2,1)S(1)}, u32[]{:S(2)}) copy-start(bf16[256,960]{0,1:T(8,128)(2,1)S(1)} %get-tuple-element.79) | copy-start | bytes 1474564
  343.7 14.4 %collective-permute-start.1 = (bf16[256,960]{0,1:T(8,128)(2,1)S(1)}, bf16[256,960]{0,1:T(8,128)(2,1)S(1)}, u32[]{:S(2)}, u32[]{:S(2)}) collective-permute-start(bf16[256,960]{0,1:T(8,128)(2,1)S(1)} %get-tuple-element.79), channel_id=1, source_target_pairs={{0,16},{1,17},{2,18},{3,19},{4,20},{5,21},{6,22},{7,23},{8,24},{9,... | collective-permute-start | bytes 1474568 | tf_op jit(solution)/shard_map/ppermute | solution.py:25
  364.5 115.9 %reduce-scatter.6.cloned.1.call-start = ((), (), s32[]{:S(2)}) async-start(), calls=%async_computation.9 | async-start | bytes 2949120 | tf_op jit(solution)/shard_map/reduce_scatter | solution.py:289
  400.3 10.0 %copy-start.26 = (bf16[1,8,120,480]{3,2,0,1:T(8,128)(2,1)S(1)}, bf16[1,8,120,480]{3,2,0,1:T(8,128)(2,1)}, u32[]{:S(2)}) copy-start(bf16[1,8,120,480]{3,2,0,1:T(8,128)(2,1)} %get-tuple-element.104) | copy-start | bytes 2764804
  400.3 10.5 %copy-start.31 = (bf16[1,8,120,480]{3,2,0,1:T(8,128)(2,1)S(1)}, bf16[1,8,120,480]{3,2,0,1:T(8,128)(2,1)}, u32[]{:S(2)}) copy-start(bf16[1,8,120,480]{3,2,0,1:T(8,128)(2,1)} %get-tuple-element.103) | copy-start | bytes 2764804
  413.1 201.5 %copy-start.170 = (f32[256]{0:T(256)}, f32[256]{0:T(256)S(1)}, u32[]{:S(2)}) copy-start(f32[256]{0:T(256)S(1)} %get-tuple-element.63) | copy-start | bytes 3076
  413.1 201.6 %copy-start.180 = (f32[256]{0:T(256)}, f32[256]{0:T(256)S(1)}, u32[]{:S(2)}) copy-start(f32[256]{0:T(256)S(1)} %get-tuple-element.62) | copy-start | bytes 3076
  443.8 132.8 %reduce-scatter.8.cloned.1.call-start = ((), (), s32[]{:S(2)}) async-start(), calls=%async_computation.10 | async-start | bytes 2949120 | tf_op jit(solution)/shard_map/reduce_scatter | solution.py:289
  444.2 38.3 %copy-start.189 = (pred[320]{0:T(512)(128)(4,1)}, pred[320]{0:T(512)(128)(4,1)S(1)}, u32[]{:S(2)}) copy-start(pred[320]{0:T(512)(128)(4,1)S(1)} %fusion.180) | copy-start | bytes 964
  461.9 20.9 %copy-start.124 = (bf16[256,960]{0,1:T(8,128)(2,1)S(1)}, bf16[256,960]{0,1:T(8,128)(2,1)}, u32[]{:S(2)}) copy-start(bf16[256,960]{0,1:T(8,128)(2,1)} %fusion.63) | copy-start | bytes 1474564
  485.6 15.3 %slice-start.8 = ((s8[15728640]{0:T(1024)(128)(4,1)}), s8[4194304]{0:T(1024)(128)(4,1)S(1)}, s32[]{:S(2)}) async-start(s8[15728640]{0:T(1024)(128)(4,1)} %bitcast.439), calls=%async_computation.23 | async-start | bytes 8388608
  487.5 13.4 %slice-start.9 = ((s8[15728640]{0:T(1024)(128)(4,1)}), s8[4194304]{0:T(1024)(128)(4,1)S(1)}, s32[]{:S(2)}) async-start(s8[15728640]{0:T(1024)(128)(4,1)} %bitcast.439), calls=%async_computation.24 | async-start | bytes 8388608
  488.1 9.8 %copy-start.134 = (bf16[256,960]{0,1:T(8,128)(2,1)}, bf16[256,960]{0,1:T(8,128)(2,1)S(1)}, u32[]{:S(2)}) copy-start(bf16[256,960]{0,1:T(8,128)(2,1)S(1)} %add_convert_fusion.2) | copy-start | bytes 1474564
  488.1 12.7 %copy-start.92 = (bf16[1,2,128,960]{2,1,3,0:T(2,128)(2,1)S(1)}, bf16[1,2,128,960]{2,1,3,0:T(2,128)(2,1)}, u32[]{:S(2)}) copy-start(bf16[1,2,128,960]{2,1,3,0:T(2,128)(2,1)} %copy-done.91) | copy-start | bytes 1474564
  488.1 12.8 %slice-start.10 = ((s8[15728640]{0:T(1024)(128)(4,1)}), s8[4194304]{0:T(1024)(128)(4,1)S(1)}, s32[]{:S(2)}) async-start(s8[15728640]{0:T(1024)(128)(4,1)} %bitcast.439), calls=%async_computation.25 | async-start | bytes 8388608
  488.1 12.8 %slice-start.11 = ((s8[15728640]{0:T(1024)(128)(4,1)}), s8[3145728]{0:T(1024)(128)(4,1)S(1)}, s32[]{:S(2)}) async-start(s8[15728640]{0:T(1024)(128)(4,1)} %bitcast.439), calls=%async_computation.26 | async-start | bytes 6291456
  488.1 12.7 %collective-permute-start.2 = (bf16[256,960]{0,1:T(8,128)(2,1)S(1)}, bf16[256,960]{0,1:T(8,128)(2,1)S(1)}, u32[]{:S(2)}, u32[]{:S(2)}) collective-permute-start(bf16[256,960]{0,1:T(8,128)(2,1)S(1)} %add_convert_fusion.2), channel_id=1, source_target_pairs={{16,0},{17,1},{18,2},{19,3},{20,4},{21,5},{22,6},{23,7},{24,8},{25... | collective-permute-start | bytes 1474568 | tf_op jit(solution)/shard_map/ppermute | solution.py:25
  500.9 11.7 %copy-start.56 = (bf16[256,960]{0,1:T(8,128)(2,1)}, bf16[256,960]{0,1:T(8,128)(2,1)S(1)}, u32[]{:S(2)}) copy-start(bf16[256,960]{0,1:T(8,128)(2,1)S(1)} %bitcast_select_fusion) | copy-start | bytes 1474564
  539.8 137.3 %reduce-scatter.10.cloned.1.call-start = ((), (), s32[]{:S(2)}) async-start(), calls=%async_computation.11 | async-start | bytes 2949120 | tf_op jit(solution)/shard_map/reduce_scatter | solution.py:289
  543.8 34.9 %copy-start.190 = (pred[320]{0:T(512)(128)(4,1)S(1)}, pred[320]{0:T(512)(128)(4,1)}, u32[]{:S(2)}) copy-start(pred[320]{0:T(512)(128)(4,1)} %copy-done.189) | copy-start | bytes 964
  544.3 34.6 %copy-start.128 = (bf16[256,960]{0,1:T(8,128)(2,1)}, bf16[256,960]{0,1:T(8,128)(2,1)S(1)}, u32[]{:S(2)}) copy-start(bf16[256,960]{0,1:T(8,128)(2,1)S(1)} %fusion.66) | copy-start | bytes 1474564
  585.8 12.6 %collective-permute-start.3 = (bf16[256,960]{0,1:T(8,128)(2,1)}, bf16[256,960]{0,1:T(8,128)(2,1)S(1)}, u32[]{:S(2)}, u32[]{:S(2)}) collective-permute-start(bf16[256,960]{0,1:T(8,128)(2,1)} %get-tuple-element.59), channel_id=1, source_target_pairs={{16,0},{17,1},{18,2},{19,3},{20,4},{21,5},{22,6},{23,7},{24,8},{25... | collective-permute-start | bytes 1474568 | tf_op jit(solution)/shard_map/ppermute | solution.py:25
  640.3 163.2 %reduce-scatter.12.cloned.1.call-start = ((), (), s32[]{:S(2)}) async-start(), calls=%async_computation.12 | async-start | bytes 5849088 | tf_op jit(solution)/shard_map/reduce_scatter | solution.py:403
  659.0 25.4 %copy-start.24 = (bf16[2,1600,480]{2,1,0:T(8,128)(2,1)S(1)}, bf16[2,1600,480]{2,1,0:T(8,128)(2,1)}, u32[]{:S(2)}) copy-start(bf16[2,1600,480]{2,1,0:T(8,128)(2,1)} %copy-done.19) | copy-start | bytes 9216004
  686.5 23.6 %copy-start.118 = (f32[256,480]{0,1:T(8,128)}, f32[256,480]{0,1:T(8,128)S(1)}, u32[]{:S(2)}) copy-start(f32[256,480]{0,1:T(8,128)S(1)} %fusion.84) | copy-start | bytes 1474564
  688.0 22.0 %copy-start.120 = (f32[256,480]{0,1:T(8,128)}, f32[256,480]{0,1:T(8,128)S(1)}, u32[]{:S(2)}) copy-start(f32[256,480]{0,1:T(8,128)S(1)} %fusion.78) | copy-start | bytes 1474564
  688.0 17.2 %copy-start.136 = (bf16[768,960]{0,1:T(8,128)(2,1)S(1)}, bf16[768,960]{0,1:T(8,128)(2,1)}, u32[]{:S(2)}) copy-start(bf16[768,960]{0,1:T(8,128)(2,1)} %pad_maximum_fusion.10) | copy-start | bytes 4423684
  724.2 239.6 %reduce-scatter.14.cloned.1.call-start = ((), (), s32[]{:S(2)}) async-start(), calls=%async_computation.13 | async-start | bytes 16711680 | tf_op jit(solution)/shard_map/reduce_scatter | solution.py:376
  (200 other events, 510.0 us)
Sparse Core Ops, SparseCore 0:
  10.9 60.0 all-gather.14
  83.5 32.4 all-gather.6
  118.3 119.2 all-gather.8
  271.2 33.0 all-gather.10
  364.6 33.8 all-gather.12
  443.9 36.4 reduce-scatter.5
  539.9 36.6 reduce-scatter.7
  640.5 36.5 reduce-scatter.9
  724.3 79.0 reduce-scatter.11
  808.0 155.8 reduce-scatter.13
